TPU v7x, 32 devices: a whole 2x2x4 slice. The times are simulated.
32 devices in a mesh: row: 2 (over y), col: 16 (over z, x, core).
Axes of the slice: x: 2, y: 2, z: 4, core: 2. Of those that a mesh axis runs over, the one named last changes fastest.
Arguments:
- primal: float32 [16, 1024, 1024], P('col'), as said below
- dual_inv: float32 [16, 1024, 1024], P('col'), as said below
- col_values: bfloat16 [16, 16, 128, 4096], P(None, None, 'col'), as said below
- col_perm: int32 [16, 2048], replicated, may hold values from 0 to 2047, each once within a row
- slab_values: bfloat16 [16, 128, 4096], P('col', 'row'), as said below
- slab_tile: int32 [16, 128], P('col', 'row'), may hold values from 0 to 15
Outputs:
- schur_cyclic: float32 [128, 2048], P('row', 'col')
Inputs may be any that keep to these rules, and one draw needn't show every extreme that they name: Each block's row of col_perm names every constraint exactly once. Each block of primal is symmetric. Each block of dual_inv is symmetric. `col_values`: every tile, read row-major as 64 x 64, is symmetric. `slab_values`: every tile, read row-major as 64 x 64, is symmetric.
All inputs are finite; a program needn't handle non-finite values.
Results may differ from a plain program's by a relative error of at most 0.0021.
Values may be sent and summed in bfloat16 or wider, within the bound.
A program may use at most 256 MiB of HBM per device.

v0:
```python
import jax
import jax.numpy as jnp
from jax import lax
from jax.sharding import PartitionSpec as P

TILE = 64


HIGHEST = lax.Precision.HIGHEST


def body(primal, dual_inv, col_values, col_perm, slab_values, slab_tile):
    tile_size = TILE
    tile_count = col_values.shape[1]
    order = primal.shape[1]
    slab_rows = slab_values.shape[1]
    columns = col_perm.shape[1]
    block = lax.axis_index("col")
    slab_square = slab_values[0].reshape(slab_rows, tile_size, tile_size)
    primal_rows = jnp.take(primal[0].reshape(tile_count, tile_size, order), slab_tile[0], axis=0)
    dual_rows = jnp.take(dual_inv[0].reshape(tile_count, tile_size, order), slab_tile[0], axis=0)
    panel = jnp.einsum(
        "sac,scn->san", slab_square.astype(jnp.float32), dual_rows, precision=HIGHEST
    )
    primal_split = primal_rows.reshape(slab_rows, tile_size, tile_count, tile_size)
    panel_split = panel.reshape(slab_rows, tile_size, tile_count, tile_size)
    terms = jnp.einsum("scue,scuf->suef", primal_split, panel_split, precision=HIGHEST)
    terms = terms.reshape(slab_rows, tile_count, tile_size * tile_size).astype(jnp.bfloat16)
    empty = jnp.zeros((slab_rows, columns), jnp.float32)
    ordering = lax.dynamic_index_in_dim(col_perm, block, 0, keepdims=False)
    arrived = lax.all_to_all(col_values, "col", split_axis=0, concat_axis=2, tiled=True)
    contrib = jnp.einsum("sup,ukp->suk", terms, arrived[0], preferred_element_type=jnp.float32)
    partial_sum = empty.at[:, ordering].set(contrib.reshape(slab_rows, columns))
    summed = lax.psum_scatter(partial_sum, "col", scatter_dimension=1, tiled=True)
    return lax.all_to_all(summed, "row", split_axis=0, concat_axis=0, tiled=True)


def solution(mesh):
    return jax.shard_map(
        body,
        mesh=mesh,
        in_specs=(
            P("col", None, None),
            P("col", None, None),
            P(None, None, "col", None),
            P(),
            P("col", "row", None),
            P("col", "row"),
        ),
        out_specs=P("row", "col"),
        check_vma=False,
    )
```

profile of v0, /device:TPU:0, one launch (start us, length us, event | category | flops | bytes accessed | tf_op | source)
XLA Modules:
  0.0 467.5 jit_solution(2558385118797178635)
XLA Ops:
  6.5 0.0 copy-start
  6.5 0.0 copy-start.1
  6.5 7.5 %all-to-all-start = ((bf16[16,16,8,4096]{3,2,1,0:T(8,128)(2,1)}), bf16[16,16,8,4096]{3,2,1,0:T(8,128)(2,1)}, u32[]{:S(2)}, u32[]{:S(2)}) async-start(bf16[16,16,8,4096]{3,2,1,0:T(8,128)(2,1)} %param.10), calls=%async_computation | async-start | bytes 33554432 | tf_op jit(solution)/shard_map/all_to_all | solution.py:31
  14.1 0.0 reduce-scatter.2.cloned.1.call-start
  14.1 0.0 copy-done
  14.1 1.1 reshape_squeeze.11
  15.3 0.0 copy-done.1
  15.3 11.0 %gather_fusion.1 = f32[64,64,1024]{2,1,0:T(8,128)} fusion(f32[16,64,1024]{2,1,0:T(8,128)} %bitcast.39, s32[1024]{0:T(1024)S(1)} %pad_clamp_fusion), kind=kCustom, calls=%fused_computation.1.clone | custom fusion | bytes 33554688 | tf_op jit(solution)/shard_map/jit(_take)/gather | solution.py:21
  26.3 16.2 %fusion.10 = f32[64,64,1024]{2,1,0:T(8,128)} fusion(bf16[64,64,64]{2,1,0:T(8,128)(2,1)S(1)} %reshape_squeeze.11, f32[64,64,1024]{2,1,0:T(8,128)} %gather_fusion.1, pred[64]{0:T(512)(128)(4,1)S(1)} %compare_and_fusion), kind=kOutput, calls=%fused_computation.11 | convolution fusion | flops 3225419776 | bytes 34078784 | tf_op jit(solution)/shard_map/sac,scn->san/dot_general | solution.py:22
  42.5 25.8 %reshape.48 = f32[64,64,16,64]{3,2,1,0:T(8,128)} reshape(f32[64,64,1024]{2,1,0:T(8,128)} %fusion.10) | data formatting | bytes 33554432 | tf_op jit(solution)/shard_map/reshape | solution.py:26
  68.4 11.0 %gather_fusion = f32[64,64,1024]{2,1,0:T(8,128)} fusion(f32[16,64,1024]{2,1,0:T(8,128)} %bitcast.40, s32[1024]{0:T(1024)S(1)} %pad_clamp_fusion), kind=kCustom, calls=%fused_computation.clone | custom fusion | bytes 33554688 | tf_op jit(solution)/shard_map/jit(_take)/gather | solution.py:20
  79.4 12.2 %broadcast_select_fusion = f32[64,64,1024]{2,1,0:T(8,128)} fusion(f32[64,64,1024]{2,1,0:T(8,128)} %gather_fusion, pred[64]{0:T(512)(128)(4,1)S(1)} %compare_and_fusion), kind=kLoop, calls=%fused_computation.14 | loop fusion | flops 4194304 | bytes 33554496 | tf_op jit(solution)/shard_map/jit(_take)/select_n | solution.py:20
  91.6 22.9 %copy.12 = f32[64,64,1024]{1,2,0:T(8,128)} copy(f32[64,64,1024]{2,1,0:T(8,128)} %broadcast_select_fusion) | data formatting | bytes 33554432 | tf_op jit(solution)/shard_map/jit(_take)/select_n | solution.py:20
  114.5 51.2 %fusion.7 = bf16[64,16,64,64]{3,2,1,0:T(8,128)(2,1)} fusion(f32[64,64,16,64]{1,3,2,0:T(8,128)} %bitcast.38, f32[64,64,16,64]{3,2,1,0:T(8,128)} %reshape.48), kind=kOutput, calls=%fused_computation.10 | convolution fusion | flops 3225419776 | bytes 41943040 | tf_op jit(solution)/shard_map/scue,scuf->suef/dot_general | solution.py:27
  165.7 22.6 %convert_element_type.8 = bf16[64,16,4096]{2,1,0:T(8,128)(2,1)} reshape(bf16[64,16,64,64]{3,2,1,0:T(8,128)(2,1)} %fusion.7) | data formatting | bytes 16777216 | tf_op jit(solution)/shard_map/convert_element_type | solution.py:28
  188.3 0.9 compare_select_fusion
  189.2 121.7 %all-to-all-done = bf16[16,16,8,4096]{3,2,1,0:T(8,128)(2,1)} async-done(((bf16[16,16,8,4096]{3,2,1,0:T(8,128)(2,1)}), bf16[16,16,8,4096]{3,2,1,0:T(8,128)(2,1)}, u32[]{:S(2)}, u32[]{:S(2)}) %all-to-all-start) | async-done | bytes 16777248 | tf_op jit(solution)/shard_map/all_to_all | solution.py:31
  310.9 11.7 %fusion.16 = f32[16,8,8,128]{3,2,1,0:T(8,128)S(1)} fusion(bf16[64,16,4096]{2,1,0:T(8,128)(2,1)} %convert_element_type.8, bf16[16,16,8,4096]{3,2,1,0:T(8,128)(2,1)} %all-to-all-done), kind=kOutput, calls=%fused_computation.16 | convolution fusion | flops 1073741824 | bytes 25690112 | tf_op jit(solution)/shard_map/sup,ukp->suk/dot_general | solution.py:32
  322.6 0.3 copy.17
  322.9 6.6 %scatter_custom_fusion = f32[64,2048]{0,1:T(8,128)} fusion(s32[2048]{0:T(1024)S(1)} %bitcast.44, f32[2048,64]{1,0:T(8,128)S(1)} %copy.17, f32[]{:T(128)} %constant.5.clone.1), kind=kCustom, calls=%fused_computation.18 | custom fusion | bytes 524292 | tf_op jit(solution)/shard_map/scatter | solution.py:33
  329.5 0.0 reduce-scatter.2.cloned.1.call-update
  329.5 123.1 %reduce-scatter.2.cloned.1.call-done = f32[64,128]{0,1:T(8,128)} async-done(((f32[64,2048]{0,1:T(8,128)}), f32[64,128]{0,1:T(8,128)}) %reduce-scatter.2.cloned.1.call-update) | async-done | bytes 32784 | tf_op jit(solution)/shard_map/reduce_scatter | solution.py:34
  452.6 0.9 copy.18
  453.5 6.5 %all_to_all.27 = f32[2,32,128]{2,1,0:T(8,128)S(1)} all-to-all(f32[2,32,128]{2,1,0:T(8,128)S(1)} %bitcast.42), channel_id=1, replica_groups=mesh['row'=2,'col'=16] {'row'}, dimensions={0} | all-to-all | bytes 65536 | tf_op jit(solution)/shard_map/all_to_all | solution.py:35
  460.0 0.6 copy.37
  (4 shorter events, 0.1 us)
Async XLA Ops:
  6.5 7.6 %copy-start = (bf16[1,64,4096]{2,1,0:T(8,128)(2,1)S(1)}, bf16[1,64,4096]{2,1,0:T(8,128)(2,1)}, u32[]{:S(2)}) copy-start(bf16[1,64,4096]{2,1,0:T(8,128)(2,1)} %param.12) | copy-start | bytes 1572868
  6.5 8.7 %copy-start.1 = (s32[1,64]{1,0:T(1,128)S(1)}, s32[1,64]{1,0:T(1,128)}, u32[]{:S(2)}) copy-start(s32[1,64]{1,0:T(1,128)} %param.13) | copy-start | bytes 772
  6.5 304.3 %all-to-all-start = ((bf16[16,16,8,4096]{3,2,1,0:T(8,128)(2,1)}), bf16[16,16,8,4096]{3,2,1,0:T(8,128)(2,1)}, u32[]{:S(2)}, u32[]{:S(2)}) async-start(bf16[16,16,8,4096]{3,2,1,0:T(8,128)(2,1)} %param.10), calls=%async_computation | async-start | bytes 33554432 | tf_op jit(solution)/shard_map/all_to_all | solution.py:31
  14.1 438.5 %reduce-scatter.2.cloned.1.call-start = ((), (), s32[]{:S(2)}) async-start(), calls=%async_computation.3 | async-start | bytes 1114112 | tf_op jit(solution)/shard_map/reduce_scatter | solution.py:34
Sparse Core Ops, SparseCore 0:
  329.7 122.8 reduce-scatter.1
where the time goes:
time: 470 us; the launch traced here: 467 us
  waiting for transfers between devices  245 us (52%)
  local copies, waits for them, and re-layouts  103 us (22%)
  matrix products  79.1 us (17%)
  between operations  13.5 us (3%)
  other arithmetic  13.1 us (3%)
  starting transfers between devices  7.58 us (2%)
  blocking collectives  6.51 us (1%)
    reduce_scatter x1, waiting for transfers between devices, body(): lax.psum_scatter(partial_sum, 'col', scatter_dimension=1, tiled=True)  123 us
    all_to_all x1, waiting for transfers between devices, body(): lax.all_to_all(col_values, 'col', split_axis=0, concat_axis=2, tiled=True)  122 us
    dot_general x1, matrix products, body(): jnp.einsum('scue,scuf->suef', primal_split, panel_split, precision=HIGHEST)  51.2 us
    reshape x1, local copies, waits for them, and re-layouts, body(): panel_split = panel.reshape(slab_rows, tile_size, tile_count, tile_size)  25.8 us
    select_n x1, local copies, waits for them, and re-layouts, body(): jnp.take(primal[0].reshape(tile_count, tile_size, order), slab_tile[0], a...  22.9 us
    convert_element_type x1, local copies, waits for them, and re-layouts, body(): terms.reshape(slab_rows, tile_count, tile_size * tile_size)  22.6 us
    dot_general x1, matrix products, body(): jnp.einsum('sac,scn->san', slab_square.astype(jnp.float32), dual_rows, pr...  16.2 us
    select_n x2, other arithmetic, body(): jnp.take(primal[0].reshape(tile_count, tile_size, order), slab_tile[0], a...  12.2 us
  transfers between devices with their start and end apart: 2, of which 2 were waited for; matrix products, arithmetic and copies ran while one was open for 37% of the time, Pallas kernels for 0%

commit v1 on v0

v1 whole, which is shorter than its diff:
```python
import jax
import jax.numpy as jnp
from jax import lax
from jax.sharding import PartitionSpec as P

TILE = 64
RB = 32


HIGHEST = lax.Precision.HIGHEST


def body(n_row, primal, dual_inv, col_values, col_perm, slab_values, slab_tile):
    tile_size = TILE
    tile_count = col_values.shape[1]
    order = primal.shape[1]
    columns = col_perm.shape[1]
    block = lax.axis_index("col")
    own = lax.axis_index("row")
    part = tile_count // n_row
    width = part * tile_size
    slab = lax.all_gather(slab_values[0], "row", axis=0, tiled=True)
    tiles = lax.all_gather(slab_tile[0], "row", axis=0, tiled=True)
    slab_rows = slab.shape[0]
    mine = lax.dynamic_slice_in_dim(col_values, own * part, part, axis=1)
    arrived = lax.all_to_all(mine, "col", split_axis=0, concat_axis=2, tiled=True)
    primal_cols = lax.dynamic_slice_in_dim(primal[0], own * width, width, axis=1)
    dual_cols = lax.dynamic_slice_in_dim(dual_inv[0], own * width, width, axis=1)
    slab_square = slab.reshape(slab_rows, tile_size, tile_size)
    primal_rows = jnp.take(primal_cols.reshape(tile_count, tile_size, width), tiles, axis=0)
    dual_rows = jnp.take(dual_cols.reshape(tile_count, tile_size, width), tiles, axis=0)
    panel = jnp.einsum(
        "sac,scn->san", slab_square.astype(jnp.float32), dual_rows, precision=HIGHEST
    )
    primal_split = primal_rows.reshape(slab_rows, tile_size, part, tile_size)
    panel_split = panel.reshape(slab_rows, tile_size, part, tile_size)
    terms = jnp.einsum("scue,scuf->suef", primal_split, panel_split, precision=HIGHEST)
    terms = terms.reshape(slab_rows, part, tile_size * tile_size).astype(jnp.bfloat16)
    contrib = jnp.einsum("sup,ukp->suk", terms, arrived[0], preferred_element_type=jnp.float32)
    contrib = contrib.reshape(slab_rows // (RB * n_row), n_row, RB, columns // n_row)
    contrib = jnp.transpose(contrib, (1, 0, 2, 3)).reshape(slab_rows, columns // n_row)
    contrib = lax.all_to_all(contrib, "row", split_axis=0, concat_axis=1, tiled=True)
    ordering = lax.dynamic_index_in_dim(col_perm, block, 0, keepdims=False)
    onehot = (ordering[:, None] == jnp.arange(columns)[None, :]).astype(jnp.float32)
    placed = jnp.dot(contrib, onehot, precision=HIGHEST)
    return lax.psum_scatter(placed, "col", scatter_dimension=1, tiled=True)


def solution(mesh):
    def run(*args):
        return body(mesh.shape["row"], *args)

    return jax.shard_map(
        run,
        mesh=mesh,
        in_specs=(
            P("col", None, None),
            P("col", None, None),
            P(None, None, "col", None),
            P(),
            P("col", "row", None),
            P("col", "row"),
        ),
        out_specs=P("row", "col"),
        check_vma=False,
    )
```

time: 470 us -> 315 us (0.67)
  waiting for transfers between devices: 245 us -> 64.6 us
  local copies, waits for them, and re-layouts: 103 us -> 130 us
    all_to_all x1 -> x2, waiting for transfers between devices: 122 us -> 7.81 us  [the longest x1 7.81 us: body(): lax.all_to_all(contrib, 'row', split_axis=0, concat_axis=1, tiled=True)]
    reduce_scatter x1, waiting for transfers between devices: 123 us -> 56.1 us  [body(): return lax.psum_scatter(placed, 'col', scatter_dimension=1, tiled=True)]
    reshape x3 -> x4, local copies, waits for them, and re-layouts: 26.2 us -> 56.5 us  [the longest x1 30.5 us: body(): panel_split = panel.reshape(slab_rows, tile_size, part, tile_size)]
    select_n x1 -> x0, local copies, waits for them, and re-layouts: 22.9 us -> none  [body(): jnp.take(primal[0].reshape(tile_count, tile_size, order), slab_tile[0], a...]
    dot_general x0 -> x1, local copies, waits for them, and re-layouts: none -> 17.6 us  [body(): jnp.einsum('sac,scn->san', slab_square.astype(jnp.float32), dual_rows, pr...]
    dynamic_slice x0 -> x3, local copies, waits for them, and re-layouts: none -> 11.9 us  [the longest x1 7.84 us: body(): mine = lax.dynamic_slice_in_dim(col_values, own * part, part, axis=1)]
    dot_general x0 -> x1, matrix products: none -> 7.2 us  [body(): placed = jnp.dot(contrib, onehot, precision=HIGHEST)]
    dot_general x1, matrix products: 51.2 us -> 44.2 us  [body(): jnp.einsum('scue,scuf->suef', primal_split, panel_split, precision=HIGHEST)]
  transfers between devices with their start and end apart: 2 -> 4, of which waited for: 2 -> 2; matrix products, arithmetic and copies ran while one was open for 37% -> 62% of each run, Pallas kernels for 0% -> 0%
where the time goes in v1:
time: 315 us; the launch traced here: 312 us
  local copies, waits for them, and re-layouts  130 us (41%)
  matrix products  76.3 us (24%)
  waiting for transfers between devices  64.6 us (21%)
  between operations  14.2 us (5%)
  other arithmetic  12.2 us (4%)
  starting transfers between devices  11.2 us (4%)
  blocking collectives  4.25 us (1%)
    reduce_scatter x1, waiting for transfers between devices, body(): return lax.psum_scatter(placed, 'col', scatter_dimension=1, tiled=True)  56.1 us
    dot_general x1, matrix products, body(): jnp.einsum('scue,scuf->suef', primal_split, panel_split, precision=HIGHEST)  44.2 us
    reshape x1, local copies, waits for them, and re-layouts, body(): panel_split = panel.reshape(slab_rows, tile_size, part, tile_size)  30.5 us
    reshape x1, local copies, waits for them, and re-layouts, body(): primal_split = primal_rows.reshape(slab_rows, tile_size, part, tile_size)  22.9 us
    convert_element_type x1, local copies, waits for them, and re-layouts, body(): terms.reshape(slab_rows, part, tile_size * tile_size).astype(jnp.bfloat16)  21.6 us
    dot_general x1, local copies, waits for them, and re-layouts, body(): jnp.einsum('sac,scn->san', slab_square.astype(jnp.float32), dual_rows, pr...  17.6 us
    dot_general x1, matrix products, body(): jnp.einsum('sac,scn->san', slab_square.astype(jnp.float32), dual_rows, pr...  16.8 us
    select_n x2, other arithmetic, body(): jnp.take(primal_cols.reshape(tile_count, tile_size, width), tiles, axis=0)  12.1 us
  transfers between devices with their start and end apart: 4, of which 2 were waited for; matrix products, arithmetic and copies ran while one was open for 62% of the time, Pallas kernels for 0%

profile of v1, /device:TPU:0, one launch (start us, length us, event | category | flops | bytes accessed | tf_op | source)
XLA Modules:
  0.0 312.5 jit_solution(7240419470820501739)
XLA Ops:
  6.5 0.0 copy-start
  6.5 0.0 copy-start.2
  6.5 0.0 copy-start.1
  6.5 7.8 %constant_dynamic-slice_fusion.3 = bf16[16,8,8,4096]{3,2,1,0:T(8,128)(2,1)} fusion(bf16[16,16,8,4096]{3,2,1,0:T(8,128)(2,1)} %param.10, s32[]{:T(128)S(6)} %select_n.18), kind=kLoop, calls=%fused_computation.22 | loop fusion | bytes 16777220 | tf_op jit(solution)/shard_map/dynamic_slice | solution.py:25
  14.4 7.4 %all-to-all-start = ((bf16[16,8,8,4096]{3,2,1,0:T(8,128)(2,1)}), bf16[16,8,8,4096]{3,2,1,0:T(8,128)(2,1)}, u32[]{:S(2)}, u32[]{:S(2)}) async-start(bf16[16,8,8,4096]{3,2,1,0:T(8,128)(2,1)} %constant_dynamic-slice_fusion.3), calls=%async_computation | async-start | bytes 16777216 | tf_op jit(solution)/shard_map/all_to_all | solution.py:26
  21.8 0.0 all-gather.4.cloned.1.call-start
  21.9 0.7 all-gather.4.cloned.1.call-update
  22.5 0.0 copy-done.2
  22.6 0.6 dynamic-slice.2
  23.8 0.0 copy-done.1
  23.8 0.1 bitcast_dynamic-update-slice_fusion
  23.9 4.3 %all-reduce = s32[128]{0:T(128)S(1)} all-reduce(s32[128]{0:T(128)S(1)} %bitcast_dynamic-update-slice_fusion), channel_id=2, replica_groups=mesh['row'=2,'col'=16] {'row'}, use_global_device_ids=true, to_apply=%add | all-reduce | flops 128 | bytes 1024 | tf_op jit(solution)/shard_map/all_gather | solution.py:23
  28.2 4.0 %constant_dynamic-slice_fusion.1 = (f32[1,1024,512]{2,1,0:T(8,128)}, f32[1,1024,512]{2,1,0:T(8,128)S(1)}) fusion(f32[1,1024,1024]{2,1,0:T(8,128)} %param.9, s32[]{:T(128)S(6)} %select_n.19, f32[1,1024,1024]{2,1,0:T(8,128)} %param.8), kind=kLoop, calls=%fused_computation.20 | loop fusion | bytes 8388612 | tf_op jit(solution)/shard_map/dynamic_slice | solution.py:28
  32.2 11.5 %gather_fusion.1 = f32[128,64,512]{2,1,0:T(8,128)} fusion(f32[16,64,512]{2,1,0:T(8,128)} %bitcast.38, s32[1024]{0:T(1024)S(1)} %pad_clamp_fusion), kind=kCustom, calls=%fused_computation.1.clone | custom fusion | bytes 33554944 | tf_op jit(solution)/shard_map/jit(_take)/gather | solution.py:31
  43.7 7.3 %gather_fusion = f32[128,64,512]{2,1,0:T(8,128)} fusion(f32[16,64,512]{2,1,0:T(8,128)S(1)} %bitcast.37, s32[1024]{0:T(1024)S(1)} %pad_clamp_fusion), kind=kCustom, calls=%fused_computation.clone | custom fusion | bytes 33554944 | tf_op jit(solution)/shard_map/jit(_take)/gather | solution.py:30
  51.1 12.1 %broadcast_select_fusion = f32[128,64,512]{2,1,0:T(8,128)} fusion(f32[128,64,512]{2,1,0:T(8,128)} %gather_fusion, pred[128]{0:T(512)(128)(4,1)S(1)} %compare_and_fusion), kind=kLoop, calls=%fused_computation.12 | loop fusion | flops 4194304 | bytes 33554560 | tf_op jit(solution)/shard_map/jit(_take)/select_n | solution.py:30
  63.2 22.9 %copy.46 = f32[128,64,512]{1,2,0:T(8,128)} copy(f32[128,64,512]{2,1,0:T(8,128)} %broadcast_select_fusion) | data formatting | bytes 33554432 | tf_op jit(solution)/shard_map/reshape | solution.py:35
  86.1 0.0 all-gather.4.cloned.1.call-done
  86.1 1.6 copy.35
  87.7 3.0 copy.36
  90.7 16.8 %fusion.3 = f32[128,64,512]{2,1,0:T(8,128)} fusion(bf16[128,64,64]{2,1,0:T(8,128)(2,1)S(1)} %copy.36, f32[128,64,512]{2,1,0:T(8,128)} %gather_fusion.1, pred[128]{0:T(512)(128)(4,1)S(1)} %compare_and_fusion), kind=kOutput, calls=%fused_computation.7 | convolution fusion | flops 3225419776 | bytes 34603136 | tf_op jit(solution)/shard_map/sac,scn->san/dot_general | solution.py:32
  107.5 17.6 %copy.37 = f32[128,64,512]{0,2,1:T(8,128)} copy(f32[128,64,512]{2,1,0:T(8,128)} %fusion.3) | data formatting | bytes 33554432 | tf_op jit(solution)/shard_map/sac,scn->san/dot_general | solution.py:32
  125.1 30.5 %copy.39 = f32[128,64,8,64]{3,1,2,0:T(8,128)} copy(f32[128,64,8,64]{0,3,2,1:T(8,128)} %bitcast.39) | data formatting | bytes 33554432 | tf_op jit(solution)/shard_map/reshape | solution.py:36
  155.6 44.2 %convolution_convert_fusion = bf16[128,8,64,64]{3,2,1,0:T(8,128)(2,1)} fusion(f32[128,64,8,64]{1,3,2,0:T(8,128)} %bitcast.36, f32[128,64,8,64]{3,1,2,0:T(8,128)} %copy.39), kind=kOutput, calls=%fused_computation.6 | convolution fusion | flops 3225419776 | bytes 41943040 | tf_op jit(solution)/shard_map/scue,scuf->suef/dot_general | solution.py:37
  199.8 21.6 %copy.40 = bf16[128,8,64,64]{0,3,2,1:T(8,128)(2,1)} copy(bf16[128,8,64,64]{3,2,1,0:T(8,128)(2,1)} %convolution_convert_fusion) | data formatting | bytes 16777216 | tf_op jit(solution)/shard_map/convert_element_type | solution.py:38
  221.4 0.0 all-to-all-done
  221.4 8.1 %fusion.12 = f32[128,8,128]{0,2,1:T(8,128)S(1)} fusion(bf16[128,8,4096]{0,2,1:T(8,128)(2,1)} %bitcast.40, bf16[16,8,8,4096]{3,2,1,0:T(8,128)(2,1)} %all-to-all-done), kind=kOutput, calls=%fused_computation.15 | convolution fusion | flops 1073741824 | bytes 17301504 | tf_op jit(solution)/shard_map/sup,ukp->suk/dot_general | solution.py:39
  229.5 0.2 copy.42
  229.7 0.1 reshape.42
  229.8 0.8 copy.43
  230.7 3.5 %all-to-all-start.1 = ((f32[2,64,1024]{2,1,0:T(8,128)}), f32[2,64,1024]{2,1,0:T(8,128)S(1)}, u32[]{:S(2)}, u32[]{:S(2)}) async-start(f32[2,64,1024]{2,1,0:T(8,128)} %bitcast.15), calls=%async_computation.1 | async-start | bytes 1048576 | tf_op jit(solution)/shard_map/all_to_all | solution.py:42
  234.2 0.3 reduce-scatter.2.cloned.1.call-start
  234.4 0.0 copy-done
  234.5 7.8 %all-to-all-done.1 = f32[2,64,1024]{2,1,0:T(8,128)S(1)} async-done(((f32[2,64,1024]{2,1,0:T(8,128)}), f32[2,64,1024]{2,1,0:T(8,128)S(1)}, u32[]{:S(2)}, u32[]{:S(2)}) %all-to-all-start.1) | async-done | bytes 524320 | tf_op jit(solution)/shard_map/all_to_all | solution.py:42
  242.3 7.2 %fusion.2 = f32[64,2048]{1,0:T(8,128)} fusion(f32[64,2048]{1,0:T(8,128)S(1)} %bitcast.44, s32[2048]{0:T(1024)S(1)} %bitcast.45), kind=kOutput, calls=%fused_computation.5 | convolution fusion | flops 3225419776 | bytes 1056768 | tf_op jit(solution)/shard_map/dot_general | solution.py:45
  249.5 0.0 reduce-scatter.2.cloned.1.call-update
  249.5 56.1 %reduce-scatter.2.cloned.1.call-done = f32[64,128]{1,0:T(8,128)} async-done(((f32[64,2048]{1,0:T(8,128)}), f32[64,128]{1,0:T(8,128)}) %reduce-scatter.2.cloned.1.call-update) | async-done | bytes 32784 | tf_op jit(solution)/shard_map/reduce_scatter | solution.py:46
  (6 shorter events, 0.1 us)
Async XLA Ops:
  6.5 227.9 %copy-start = (s32[16,2048]{1,0:T(8,128)S(1)}, s32[16,2048]{1,0:T(8,128)}, u32[]{:S(2)}) copy-start(s32[16,2048]{1,0:T(8,128)} %param.11) | copy-start | bytes 393220
  6.5 16.0 %copy-start.2 = (u32[32]{0:T(128)S(1)}, u32[32]{0:T(128)}, u32[]{:S(2)}) copy-start(u32[32]{0:T(128)} %constant.42) | copy-start | bytes 388
  6.5 17.3 %copy-start.1 = (s32[1,64]{1,0:T(1,128)S(1)}, s32[1,64]{1,0:T(1,128)}, u32[]{:S(2)}) copy-start(s32[1,64]{1,0:T(1,128)} %param.13) | copy-start | bytes 772
  14.4 207.0 %all-to-all-start = ((bf16[16,8,8,4096]{3,2,1,0:T(8,128)(2,1)}), bf16[16,8,8,4096]{3,2,1,0:T(8,128)(2,1)}, u32[]{:S(2)}, u32[]{:S(2)}) async-start(bf16[16,8,8,4096]{3,2,1,0:T(8,128)(2,1)} %constant_dynamic-slice_fusion.3), calls=%async_computation | async-start | bytes 16777216 | tf_op jit(solution)/shard_map/all_to_all | solution.py:26
  21.8 64.3 %all-gather.4.cloned.1.call-start = ((), (), s32[]{:S(2)}) async-start(), calls=%async_computation.4 | async-start | bytes 1572864 | tf_op jit(solution)/shard_map/all_gather | solution.py:22
  230.7 11.6 %all-to-all-start.1 = ((f32[2,64,1024]{2,1,0:T(8,128)}), f32[2,64,1024]{2,1,0:T(8,128)S(1)}, u32[]{:S(2)}, u32[]{:S(2)}) async-start(f32[2,64,1024]{2,1,0:T(8,128)} %bitcast.15), calls=%async_computation.1 | async-start | bytes 1048576 | tf_op jit(solution)/shard_map/all_to_all | solution.py:42
  234.2 71.5 %reduce-scatter.2.cloned.1.call-start = ((), (), s32[]{:S(2)}) async-start(), calls=%async_computation.3 | async-start | bytes 557056 | tf_op jit(solution)/shard_map/reduce_scatter | solution.py:46
Sparse Core Ops, SparseCore 0:
  24.2 22.5 all-gather.3
  249.7 55.9 reduce-scatter.1

commit v2 on v0

v2 whole, which is shorter than its diff:
```python
import functools

import jax
import jax.numpy as jnp
from jax import lax
from jax.experimental import pallas as pl
from jax.experimental.pallas import tpu as pltpu
from jax.sharding import PartitionSpec as P

TILE = 64
HALF = TILE // 2
RB = 32
LANES = 128
GROUP = 16
ROLL = LANES - HALF
TOGETHER = 4
MESH = pl.DeviceIdType.MESH
NT = (((1,), (1,)), ((), ()))


def split(value):
    high = value.astype(jnp.bfloat16)
    low = (value - high.astype(jnp.float32)).astype(jnp.bfloat16)
    return high, low


def kernel(
    n_row, n_col, tiles_ref, x_ref, z_ref, s_ref, perm_ref, col_ref, out_ref,
    raw, send, recv, slab, folded, corner, left, mine, theirs, hot, placed, arrived,
    load_sem, c_send, c_recv, s_send, s_recv, y_send, y_recv, p_send, p_recv,
):
    me = lax.axis_index("col")
    own = lax.axis_index("row")
    s_dev = s_ref.shape[0]
    rows = n_row * s_dev
    groups = raw.shape[1]
    pairs = groups
    flat = groups * GROUP
    packed_tiles = TILE * TILE // 2 // LANES
    slots = perm_ref.shape[2]
    columns = hot.shape[1]

    barrier = pltpu.get_barrier_semaphore()
    for k in range(1, n_col):
        pl.semaphore_signal(barrier, inc=1, device_id={"col": lax.rem(me + k, n_col)}, device_id_type=MESH)
    for k in range(1, n_row):
        pl.semaphore_signal(barrier, inc=1, device_id={"row": lax.rem(own + k, n_row)}, device_id_type=MESH)
    pl.semaphore_wait(barrier, n_col + n_row - 2)

    def offset(n):
        return n_col // 2 + lax.div(n + 1, 2) * (1 - 2 * lax.rem(n, 2))

    def target(n):
        return lax.rem(me + offset(n), n_col)

    def load(n):
        slot = lax.rem(n, 2)
        return pltpu.make_async_copy(
            col_ref.at[target(n), pl.ds(own * groups, groups)], raw.at[slot], load_sem.at[slot]
        )

    def row_copy(src, dst, out_sem, in_sem, there, here):
        return pltpu.make_async_remote_copy(
            src_ref=src, dst_ref=dst.at[here], send_sem=out_sem.at[there], recv_sem=in_sem.at[here],
            device_id={"row": there}, device_id_type=MESH,
        )

    def c_copy(there, here):
        return pltpu.make_async_remote_copy(
            src_ref=send.at[there], dst_ref=recv.at[:, pl.ds(here * GROUP, GROUP)],
            send_sem=c_send.at[there], recv_sem=c_recv.at[here],
            device_id={"col": there}, device_id_type=MESH,
        )

    def p_copy(there, here):
        return pltpu.make_async_remote_copy(
            src_ref=placed.at[there], dst_ref=arrived.at[here],
            send_sem=p_send.at[there], recv_sem=p_recv.at[here],
            device_id={"col": there}, device_id_type=MESH,
        )

    for k in range(1, n_row):
        row_copy(s_ref, slab, s_send, s_recv, lax.rem(own + k, n_row), own).start()

    lane = lax.broadcasted_iota(jnp.int32, (flat, LANES), 1)
    odd = jnp.where(lane >= TILE, 1, 0)
    entry = lane - odd * TILE

    def pack(slot, store):
        rest = jnp.zeros((flat, LANES), jnp.float32)
        for j in range(packed_tiles):
            upper = raw[slot, :, :, j * LANES:(j + 1) * LANES].astype(jnp.float32).reshape(flat, LANES)
            start = (packed_tiles + j) * LANES
            lower = raw[slot, :, :, start:start + LANES].astype(jnp.float32).reshape(flat, LANES)
            row = odd + 2 * j
            both = jnp.where(entry >= row, upper, pltpu.roll(lower, ROLL, 1))
            store(j, both.astype(jnp.bfloat16).reshape(groups, GROUP, LANES))
            rest = jnp.where(entry == row + HALF, lower, rest)
        store(packed_tiles, rest.astype(jnp.bfloat16).reshape(groups, GROUP, LANES))

    load(0).start()

    def outgoing(n, carry):
        load(n + 1).start()
        load(n).wait()
        there = target(n)

        def store(j, value):
            send[there, :, :, j * LANES:(j + 1) * LANES] = value

        pack(lax.rem(n, 2), store)
        c_copy(there, me).start()
        return carry

    lax.fori_loop(0, n_col - 1, outgoing, 0)
    load(n_col - 1).wait()

    def keep(j, value):
        recv[:, pl.ds(pl.multiple_of(me * GROUP, GROUP), GROUP), j * LANES:(j + 1) * LANES] = value

    pack((n_col - 1) % 2, keep)

    slab[own] = s_ref[...]

    wide = lax.broadcasted_iota(jnp.int32, (TILE, LANES), 1)
    first = wide < TILE
    e = lax.broadcasted_iota(jnp.int32, (HALF, LANES), 0)
    f = lax.broadcasted_iota(jnp.int32, (HALF, LANES), 1)
    f = jnp.where(f >= TILE, f - TILE, f)

    def terms(n):
        there = lax.rem(own + lax.div(n, s_dev), n_row)
        inner = lax.rem(n, s_dev)
        i = there * s_dev + inner
        t = tiles_ref[i]
        panel = jnp.dot(slab[there, inner], z_ref[t], preferred_element_type=jnp.float32)
        high, low = split(panel)
        right = jnp.concatenate([high, low, high, low], axis=0)
        for v in range(pairs):
            cut = slice(v * LANES, (v + 1) * LANES)
            term = jnp.dot(x_ref[t, cut], right[:, cut], preferred_element_type=jnp.float32)
            term = term.astype(jnp.bfloat16).astype(jnp.float32)
            term = term + term.T
            term = jnp.where(first, term[:TILE], term[TILE:])
            upper, lower = term[:HALF], term[HALF:]
            both = jnp.where(f > e, upper, jnp.where(f < e, pltpu.roll(lower, ROLL, 1), 0.5 * upper))
            folded[pl.ds(pl.multiple_of((v * rows + i) * HALF, HALF), HALF), :] = both
            rest = jnp.sum(jnp.where(f == e + HALF, 0.5 * lower, 0.0), axis=0, keepdims=True)
            corner[pl.ds(v * rows + i, 1), :] = rest

    def several(n, carry):
        for k in range(TOGETHER):
            terms(n * TOGETHER + k)
        return carry

    lax.fori_loop(0, s_dev // TOGETHER, several, 0)
    for k in range(1, n_row):
        there = lax.rem(own + k, n_row)
        row_copy(s_ref, slab, s_send, s_recv, there, there).wait_recv()
    lax.fori_loop(s_dev // TOGETHER, rows // TOGETHER, several, 0)

    near = lax.broadcasted_iota(jnp.int32, (LANES, LANES), 1) < TILE
    chunks = rows // LANES

    def lay(n, carry):
        v = lax.div(n, chunks)
        chunk = lax.rem(n, chunks)
        base = (v * rows + chunk * LANES) * HALF
        for j in range(packed_tiles + 1):
            if j < packed_tiles:
                a = folded[pl.ds(base + 2 * j, LANES, stride=HALF), :]
                b = folded[pl.ds(base + 2 * j + 1, LANES, stride=HALF), :]
            else:
                a = b = corner[pl.ds(pl.multiple_of(v * rows + chunk * LANES, LANES), LANES), :]
            u0 = jnp.where(near, a, pltpu.roll(b, TILE, 1))
            u1 = jnp.where(near, pltpu.roll(a, TILE, 1), b)
            parts = split(u0) + split(u1)
            for k, value in enumerate(parts):
                at = pl.multiple_of(k * rows + chunk * LANES, LANES)
                left[v, pl.ds(at, LANES), j * LANES:(j + 1) * LANES] = value
        return carry

    lax.fori_loop(0, pairs * chunks, lay, 0)

    column = lax.broadcasted_iota(jnp.int32, (LANES, slots), 0)
    for r in range(n_row):

        def mark(n, carry):
            start = pl.multiple_of(n * LANES, LANES)
            value = jnp.where(column + n * LANES == perm_ref[r], 1.0, 0.0)
            hot[r, pl.ds(start, LANES), :] = value.astype(jnp.bfloat16)
            return carry

        lax.fori_loop(0, columns // LANES, mark, 0)

    def landed(n, carry):
        there = target(n)
        c_copy(there, there).wait_recv()
        return carry

    lax.fori_loop(0, n_col - 1, landed, 0)

    across = n_col * GROUP
    even = lax.rem(lax.broadcasted_iota(jnp.int32, (rows, across), 1), GROUP) < GROUP // 2
    for v in range(pairs):
        both = lax.dot_general(left[v], recv[v], NT, preferred_element_type=jnp.float32)
        u0 = both[:rows] + both[rows:2 * rows]
        u1 = both[2 * rows:3 * rows] + both[3 * rows:]
        value = jnp.where(even, u0, u1)
        for block in range(rows // RB):
            q, r = divmod(block, n_row)
            mine[r, q * RB:(q + 1) * RB, v * across:(v + 1) * across] = value[block * RB:(block + 1) * RB]

    for k in range(1, n_row):
        there = lax.rem(own + k, n_row)
        row_copy(mine.at[there], theirs, y_send, y_recv, there, own).start()
    theirs[own] = mine[own]

    def place(r, total):
        high, low = split(theirs[r])
        value = jnp.concatenate([high, low], axis=0)
        value = lax.dot_general(value, hot[r], NT, preferred_element_type=jnp.float32)
        value = value[:s_dev] + value[s_dev:]
        return value if total is None else total + value

    total = place(own, None)
    for k in range(1, n_row):
        there = lax.rem(own + k, n_row)
        row_copy(mine.at[there], theirs, y_send, y_recv, there, there).wait_recv()
        total = place(there, total)
    out_cols = columns // n_col
    for c in range(n_col):
        placed[c] = total[:, c * out_cols:(c + 1) * out_cols]

    def give(n, carry):
        p_copy(target(n), me).start()
        return carry

    lax.fori_loop(0, n_col - 1, give, 0)
    summed = placed[me]
    for k in range(1, n_col):
        there = lax.rem(me + k, n_col)
        p_copy(there, there).wait_recv()
        summed = summed + arrived[there]
    out_ref[...] = summed

    def done(n, carry):
        there = target(n)
        c_copy(there, me).wait_send()
        p_copy(there, me).wait_send()
        return carry

    lax.fori_loop(0, n_col - 1, done, 0)
    for k in range(1, n_row):
        there = lax.rem(own + k, n_row)
        row_copy(s_ref, slab, s_send, s_recv, there, own).wait_send()
        row_copy(mine.at[there], theirs, y_send, y_recv, there, own).wait_send()


def halves(value):
    high = lax.reduce_precision(value, 8, 7)
    low = value - high
    return high.astype(jnp.bfloat16), low.astype(jnp.bfloat16)


def body(n_row, n_col, primal, dual_inv, col_values, col_perm, slab_values, slab_tile):
    tile_count = col_values.shape[1]
    order = primal.shape[1]
    columns = col_perm.shape[1]
    s_dev = slab_values.shape[1]
    rows = n_row * s_dev
    keep = col_values.shape[2]
    block = lax.axis_index("col")
    own = lax.axis_index("row")
    part = tile_count // n_row
    width = part * TILE
    slots = columns // n_row
    tiles = lax.all_gather(slab_tile[0], "row", axis=0, tiled=True)

    x = lax.dynamic_slice_in_dim(primal[0], own * width, width, axis=0)
    x = jnp.transpose(x.reshape(width, order // TILE, TILE), (1, 0, 2))
    high, low = halves(x)
    x = jnp.concatenate([high, high, low, low], axis=2)
    z = lax.dynamic_slice_in_dim(dual_inv[0], own * width, width, axis=1)
    high, low = halves(z.reshape(order // TILE, TILE, width))
    z = jnp.concatenate([high, low], axis=1)
    s = slab_values[0].reshape(s_dev, TILE, TILE)
    s = jnp.concatenate([s, s], axis=2)
    perm = lax.dynamic_index_in_dim(col_perm, block, 0, keepdims=False)
    perm = perm.reshape(n_row, part // 2, 2, n_col, keep)
    perm = jnp.transpose(perm, (0, 1, 3, 2, 4)).reshape(n_row, 1, slots)
    col = col_values.reshape(n_col, tile_count * keep // GROUP, GROUP, TILE * TILE)

    groups = part * keep // GROUP
    packed = TILE * TILE // 2 + LANES
    vmem = pl.BlockSpec(memory_space=pltpu.VMEM)
    dma = pltpu.SemaphoreType.DMA
    f32, bf16 = jnp.float32, jnp.bfloat16
    return pl.pallas_call(
        functools.partial(kernel, n_row, n_col),
        out_shape=jax.ShapeDtypeStruct((s_dev, columns // n_col), f32),
        in_specs=[
            pl.BlockSpec(memory_space=pltpu.SMEM), vmem, vmem, vmem, vmem,
            pl.BlockSpec(memory_space=pl.ANY),
        ],
        out_specs=vmem,
        scratch_shapes=[
            pltpu.VMEM((2, groups, GROUP, TILE * TILE), bf16),
            pltpu.VMEM((n_col, groups, GROUP, packed), bf16),
            pltpu.VMEM((groups, n_col * GROUP, packed), bf16),
            pltpu.VMEM((n_row, s_dev, TILE, 2 * TILE), bf16),
            pltpu.VMEM((groups * rows * HALF, LANES), f32),
            pltpu.VMEM((groups * rows, LANES), f32),
            pltpu.VMEM((groups, 4 * rows, packed), bf16),
            pltpu.VMEM((n_row, s_dev, slots), f32),
            pltpu.VMEM((n_row, s_dev, slots), f32),
            pltpu.VMEM((n_row, columns, slots), bf16),
            pltpu.VMEM((n_col, s_dev, columns // n_col), f32),
            pltpu.VMEM((n_col, s_dev, columns // n_col), f32),
            dma((2,)), dma((n_col,)), dma((n_col,)), dma((n_row,)), dma((n_row,)),
            dma((n_row,)), dma((n_row,)), dma((n_col,)), dma((n_col,)),
        ],
        compiler_params=pltpu.CompilerParams(
            collective_id=0, has_side_effects=True, vmem_limit_bytes=60 * 1024 * 1024
        ),
    )(tiles, x, z, s, perm, col)


def solution(mesh):
    def run(*args):
        return body(mesh.shape["row"], mesh.shape["col"], *args)

    return jax.shard_map(
        run,
        mesh=mesh,
        in_specs=(
            P("col", None, None),
            P("col", None, None),
            P(None, None, "col", None),
            P(),
            P("col", "row", None),
            P("col", "row"),
        ),
        out_specs=P("row", "col"),
        check_vma=False,
    )
```

time: 470 us -> 159 us (0.34)
  waiting for transfers between devices: 245 us -> 0 us
  Pallas kernels: 0 us -> 128 us
  local copies, waits for them, and re-layouts: 103 us -> 13.5 us
  matrix products: 79.1 us -> 0 us
  between operations: 13.5 us -> 0.74 us
  starting transfers between devices: 7.58 us -> 0 us
    pallas_call x0 -> x1, Pallas kernels: none -> 128 us  [body(): pl.pallas_call(functools.partial(kernel, n_row, n_col), out_shape=jax.Sha...]
    reduce_scatter x1 -> x0, waiting for transfers between devices: 123 us -> none  [body(): lax.psum_scatter(partial_sum, 'col', scatter_dimension=1, tiled=True)]
    all_to_all x1 -> x0, waiting for transfers between devices: 122 us -> none  [body(): lax.all_to_all(col_values, 'col', split_axis=0, concat_axis=2, tiled=True)]
    dot_general x3 -> x0, matrix products: 79.1 us -> none  [the longest x1 51.2 us: body(): jnp.einsum('scue,scuf->suef', primal_split, panel_split, precision=HIGHEST)]
    select_n x1 -> x0, local copies, waits for them, and re-layouts: 22.9 us -> none  [body(): jnp.take(primal[0].reshape(tile_count, tile_size, order), slab_tile[0], a...]
    reshape x3, local copies, waits for them, and re-layouts: 26.2 us -> 3.6 us  [the longest x1 2.7 us: body(): x = jnp.transpose(x.reshape(width, order // TILE, TILE), (1, 0, 2))]
    convert_element_type x1 -> x0, local copies, waits for them, and re-layouts: 22.6 us -> none  [body(): terms.reshape(slab_rows, tile_count, tile_size * tile_size)]
    gather x2 -> x0, local copies, waits for them, and re-layouts: 22 us -> none  [the longest x1 11 us: body(): jnp.take(primal[0].reshape(tile_count, tile_size, order), slab_tile[0], a...]
  transfers between devices with their start and end apart: 2 -> 0, of which waited for: 2 -> 0; matrix products, arithmetic and copies ran while one was open for 37% -> 0% of each run, Pallas kernels for 0% -> 0%
where the time goes in v2:
time: 159 us
  Pallas kernels  128 us (81%)
  local copies, waits for them, and re-layouts  13.5 us (8%)
  other arithmetic  11.1 us (7%)
  blocking collectives  5.75 us (4%)
    pallas_call x1, Pallas kernels, body(): pl.pallas_call(functools.partial(kernel, n_row, n_col), out_shape=jax.Sha...  128 us
    all_gather x1, blocking collectives, body(): tiles = lax.all_gather(slab_tile[0], 'row', axis=0, tiled=True)  5.75 us
    unnamed x11, local copies, waits for them, and re-layouts  5.34 us
    concatenate x1, other arithmetic, body(): x = jnp.concatenate([high, high, low, low], axis=2)  4.39 us
    convert_element_type x2, other arithmetic, halves(): return (high.astype(jnp.bfloat16), low.astype(jnp.bfloat16))  3.68 us
    dynamic_slice x1, local copies, waits for them, and re-layouts, body(): x = lax.dynamic_slice_in_dim(primal[0], own * width, width, axis=0)  3.19 us

profile of v2, /device:TPU:0, one launch (start us, length us, event | category | flops | bytes accessed | tf_op | source)
XLA Modules:
  0.0 158.8 jit_solution(14585041151791834516)
XLA Ops:
  0.0 0.0 copy-start
  0.0 1.3 dynamic-slice.2
  1.9 0.8 bitcast_dynamic-update-slice_fusion
  2.7 5.8 %all-reduce.tiles_ref = s32[128]{0:T(128)} all-reduce(s32[128]{0:T(128)S(1)} %bitcast_dynamic-update-slice_fusion), channel_id=2, replica_groups=mesh['row'=2,'col'=16] {'row'}, use_global_device_ids=true, to_apply=%add | all-reduce | flops 128 | bytes 1024 | tf_op jit(solution)/shard_map/all_gather | solution.py:278
  8.4 3.2 %constant_dynamic-slice_fusion.1 = f32[1,512,1024]{2,1,0:T(8,128)} fusion(f32[1,1024,1024]{2,1,0:T(8,128)} %param.6, s32[]{:T(128)S(6)} %select_n.8), kind=kLoop, calls=%fused_computation.11 | loop fusion | bytes 4194308 | tf_op jit(solution)/shard_map/dynamic_slice | solution.py:280
  11.6 1.9 %copy.11 = f32[1,512,1024]{1,2,0:T(8,128)S(1)} copy(f32[1,512,1024]{2,1,0:T(8,128)} %constant_dynamic-slice_fusion.1) | data formatting | bytes 4194304
  13.6 2.7 %copy.8 = f32[512,16,64]{2,0,1:T(8,128)} copy(f32[512,16,64]{0,2,1:T(8,128)S(1)} %bitcast.11) | data formatting | bytes 4194304 | tf_op jit(solution)/shard_map/reshape | solution.py:281
  16.3 3.2 %reduce-precision_convert_fusion = (bf16[16,512,64]{2,1,0:T(8,128)(2,1)S(1)}, bf16[16,512,64]{2,1,0:T(8,128)(2,1)S(1)}) fusion(f32[512,16,64]{2,0,1:T(8,128)} %copy.8), kind=kLoop, calls=%fused_computation.1 | loop fusion | flops 2097152 | bytes 4194304 | tf_op jit(solution)/shard_map/convert_element_type | solution.py:263
  19.5 0.0 copy-start.1
  19.5 4.4 %pad_maximum_fusion.x_ref = bf16[16,512,256]{2,1,0:T(8,128)(2,1)} fusion(bf16[16,512,64]{2,1,0:T(8,128)(2,1)S(1)} %get-tuple-element.6, bf16[16,512,64]{2,1,0:T(8,128)(2,1)S(1)} %get-tuple-element.5), kind=kLoop, calls=%fused_computation.3 | loop fusion | flops 16777216 | bytes 6291456 | tf_op jit(solution)/shard_map/concatenate | solution.py:283
  23.9 0.0 copy-done.1
  23.9 0.2 constant_dynamic-slice_fusion
  24.1 0.0 copy-start.2
  24.1 0.4 reduce-precision_convert_fusion.1
  24.5 1.5 pad_maximum_fusion.1.z_ref
  26.0 0.0 copy-done.2
  26.0 1.1 reshape_squeeze.3
  27.2 1.6 %pad_maximum_fusion.2.s_ref = bf16[64,64,128]{2,1,0:T(8,128)(2,1)} fusion(bf16[64,64,64]{2,1,0:T(8,128)(2,1)S(1)} %reshape_squeeze.3), kind=kLoop, calls=%fused_computation.8 | loop fusion | flops 2097152 | bytes 1572864 | tf_op jit(solution)/shard_map/concatenate | solution.py:288
  28.7 0.0 copy-done
  28.8 0.1 reshape.22
  28.9 0.1 copy.9
  29.0 0.8 reshape.32.perm_ref
  29.8 127.7 %shard_map.64 = f32[64,128]{1,0:T(8,128)} custom-call(s32[128]{0:T(128)} %all-reduce.tiles_ref, bf16[16,512,256]{2,1,0:T(8,128)(2,1)} %pad_maximum_fusion.x_ref, bf16[16,128,512]{2,1,0:T(8,128)(2,1)} %pad_maximum_fusion.1.z_ref, bf16[64,64,128]{2,1,0:T(8,128)(2,1)} %pad_maximum_fusion.2.s_ref, s32[2,1,1024]{2,1,0:T(1,128)} %reshape.32.perm_ref, ...), custom_call_target="tpu_custom_call" | custom-call | tf_op jit(solution)/shard_map/pallas_call | solution.py:299
  157.4 1.4 copy.14
  (2 shorter events, 0.0 us)
Async XLA Ops:
  0.0 28.7 %copy-start = (s32[16,2048]{1,0:T(8,128)S(1)}, s32[16,2048]{1,0:T(8,128)}, u32[]{:S(2)}) copy-start(s32[16,2048]{1,0:T(8,128)} %param.9) | copy-start | bytes 393220
  19.5 4.4 %copy-start.1 = (f32[1,1024,1024]{2,1,0:T(8,128)S(1)}, f32[1,1024,1024]{2,1,0:T(8,128)}, u32[]{:S(2)}) copy-start(f32[1,1024,1024]{2,1,0:T(8,128)} %param.7) | copy-start | bytes 12582916
  24.1 1.9 %copy-start.2 = (bf16[1,64,4096]{2,1,0:T(8,128)(2,1)S(1)}, bf16[1,64,4096]{2,1,0:T(8,128)(2,1)}, u32[]{:S(2)}) copy-start(bf16[1,64,4096]{2,1,0:T(8,128)(2,1)} %param.10) | copy-start | bytes 1572868

commit v3 on v2

v3 whole, which is shorter than its diff:
```python
import functools

import jax
import jax.numpy as jnp
from jax import lax
from jax.experimental import pallas as pl
from jax.experimental.pallas import tpu as pltpu
from jax.sharding import PartitionSpec as P

TILE = 64
HALF = TILE // 2
RB = 32
LANES = 128
GROUP = 16
ROLL = LANES - HALF
TOGETHER = 4
MESH = pl.DeviceIdType.MESH
NT = (((1,), (1,)), ((), ()))


def split(value):
    high = value.astype(jnp.bfloat16)
    low = (value - high.astype(jnp.float32)).astype(jnp.bfloat16)
    return high, low


def kernel(
    n_row, n_col, own_tile, tile_ref, perm_ref, x_hbm, z_hbm, s_hbm, col_ref, out_ref,
    x_raw, z_raw, x_ref, z_ref, tile_out, tile_in, tile_all, s_raw, slab,
    raw, send, recv, folded, corner, left, mine, theirs, hot, total, placed, arrived,
    load_sem, in_sem, c_send, c_recv, s_send, s_recv, t_send, t_recv, y_send, y_recv, p_send, p_recv,
):
    me = lax.axis_index("col")
    own = lax.axis_index("row")
    s_dev = s_hbm.shape[1]
    rows = n_row * s_dev
    pairs = send.shape[1]
    width = pairs * LANES
    packed_tiles = TILE * TILE // 2 // LANES
    across = n_col * GROUP
    columns = hot.shape[2]

    x_copy = pltpu.make_async_copy(x_hbm.at[0, pl.ds(own * width, width)], x_raw, in_sem.at[0])
    z_copy = pltpu.make_async_copy(
        z_hbm.at[0, :, pl.ds(pl.multiple_of(own * width, LANES), width)], z_raw, in_sem.at[1]
    )
    s_copy = pltpu.make_async_copy(s_hbm.at[0], s_raw.at[own], in_sem.at[2])
    x_copy.start()
    z_copy.start()
    s_copy.start()

    def offset(n):
        return n_col // 2 + lax.div(n + 1, 2) * (1 - 2 * lax.rem(n, 2))

    def target(n):
        return lax.rem(me + offset(n), n_col)

    def load(n):
        slot = lax.rem(n, 2)
        return pltpu.make_async_copy(
            col_ref.at[target(lax.rem(n, n_col)), own * pairs + lax.div(n, n_col)],
            raw.at[slot], load_sem.at[slot],
        )

    load(0).start()

    barrier = pltpu.get_barrier_semaphore()
    for k in range(1, n_col):
        pl.semaphore_signal(barrier, inc=1, device_id={"col": lax.rem(me + k, n_col)}, device_id_type=MESH)
    for k in range(1, n_row):
        pl.semaphore_signal(barrier, inc=1, device_id={"row": lax.rem(own + k, n_row)}, device_id_type=MESH)

    tile_out[...] = jnp.zeros_like(tile_out)
    tile_out[0:1, 0:s_dev] = tile_ref[...]
    pl.semaphore_wait(barrier, n_col + n_row - 2)

    def row_copy(src, dst, out_sem, in_sem, there):
        return pltpu.make_async_remote_copy(
            src_ref=src, dst_ref=dst, send_sem=out_sem, recv_sem=in_sem,
            device_id={"row": there}, device_id_type=MESH,
        )

    def tile_copy(there, here):
        return row_copy(tile_out, tile_in.at[here], t_send.at[there], t_recv.at[here], there)

    def slab_copy(there, here):
        return row_copy(s_hbm.at[0], s_raw.at[here], s_send.at[there], s_recv.at[here], there)

    def y_copy(v, there, here):
        return row_copy(
            mine.at[v, there], theirs.at[v, here], y_send.at[v, there], y_recv.at[v, here], there
        )

    def c_copy(v, there, here):
        return pltpu.make_async_remote_copy(
            src_ref=send.at[there, v], dst_ref=recv.at[v, pl.ds(here * GROUP, GROUP)],
            send_sem=c_send.at[v, there], recv_sem=c_recv.at[v, here],
            device_id={"col": there}, device_id_type=MESH,
        )

    def p_copy(there, here):
        return pltpu.make_async_remote_copy(
            src_ref=placed.at[there], dst_ref=arrived.at[here],
            send_sem=p_send.at[there], recv_sem=p_recv.at[here],
            device_id={"col": there}, device_id_type=MESH,
        )

    mates = [lax.rem(own + k, n_row) for k in range(1, n_row)]
    for there in mates:
        tile_copy(there, own).start()
        slab_copy(there, own).start()

    lane = lax.broadcasted_iota(jnp.int32, (GROUP, LANES), 1)
    odd = jnp.where(lane >= TILE, 1, 0)
    entry = lane - odd * TILE

    def pack(slot, store):
        rest = jnp.zeros((GROUP, LANES), jnp.float32)
        for j in range(packed_tiles):
            upper = raw[slot, :, j * LANES:(j + 1) * LANES].astype(jnp.float32)
            start = (packed_tiles + j) * LANES
            lower = raw[slot, :, start:start + LANES].astype(jnp.float32)
            row = odd + 2 * j
            both = jnp.where(entry >= row, upper, pltpu.roll(lower, ROLL, 1))
            store(j, both.astype(jnp.bfloat16))
            rest = jnp.where(entry == row + HALF, lower, rest)
        store(packed_tiles, rest.astype(jnp.bfloat16))

    steps = pairs * n_col

    def outgoing(n, carry):
        @pl.when(n + 1 < steps)
        def _():
            load(n + 1).start()

        load(n).wait()
        v = lax.div(n, n_col)
        step = lax.rem(n, n_col)
        there = target(step)

        def store(j, value):
            send[there, v, :, j * LANES:(j + 1) * LANES] = value

        pack(lax.rem(n, 2), store)

        @pl.when(step < n_col - 1)
        def _():
            c_copy(v, there, me).start()

        return carry

    lax.fori_loop(0, steps, outgoing, 0)
    for v in range(pairs):
        recv[v, pl.ds(pl.multiple_of(me * GROUP, GROUP), GROUP), :] = send[me, v]

    half = lax.broadcasted_iota(jnp.int32, (width, LANES), 1) < TILE
    x_copy.wait()
    for j in range(x_raw.shape[1] // LANES):
        a = x_raw[:, j * LANES:(j + 1) * LANES]
        b = pltpu.roll(a, TILE, 1)
        for k, value in enumerate((jnp.where(half, a, b), jnp.where(half, b, a))):
            high, low = split(value)
            x_ref[2 * j + k, :, :LANES] = high
            x_ref[2 * j + k, :, LANES:] = low
    z_copy.wait()

    def parts_of(t, carry):
        high, low = split(z_raw[pl.ds(pl.multiple_of(t * TILE, TILE), TILE), :])
        z_ref[t, :TILE] = high
        z_ref[t, TILE:] = low
        return carry

    lax.fori_loop(0, z_ref.shape[0], parts_of, 0)

    slab_half = lax.broadcasted_iota(jnp.int32, (s_dev, LANES), 1) < TILE

    def expand(r):
        for j in range(TILE * TILE // LANES):
            a = s_raw[r, :, j * LANES:(j + 1) * LANES].astype(jnp.float32)
            b = pltpu.roll(a, TILE, 1)
            slab[pl.ds(r * s_dev * TILE + 2 * j, s_dev, stride=TILE), :] = jnp.where(slab_half, a, b)
            slab[pl.ds(r * s_dev * TILE + 2 * j + 1, s_dev, stride=TILE), :] = jnp.where(slab_half, b, a)

    s_copy.wait()
    expand(own)

    wide = lax.broadcasted_iota(jnp.int32, (TILE, LANES), 1)
    first = wide < TILE
    e = lax.broadcasted_iota(jnp.int32, (HALF, LANES), 0)
    f = lax.broadcasted_iota(jnp.int32, (HALF, LANES), 1)
    f = jnp.where(f >= TILE, f - TILE, f)

    def terms(i, t):
        square = slab[pl.ds(pl.multiple_of(i * TILE, TILE), TILE), :].astype(jnp.bfloat16)
        panel = jnp.dot(square, z_ref[t], preferred_element_type=jnp.float32)
        high, low = split(panel)
        right = jnp.concatenate([high, low, high, low], axis=0)
        for v in range(pairs):
            cut = slice(v * LANES, (v + 1) * LANES)
            term = jnp.dot(x_ref[t, cut], right[:, cut], preferred_element_type=jnp.float32)
            term = term.astype(jnp.bfloat16).astype(jnp.float32)
            term = term + term.T
            term = jnp.where(first, term[:TILE], term[TILE:])
            upper, lower = term[:HALF], term[HALF:]
            both = jnp.where(f > e, upper, jnp.where(f < e, pltpu.roll(lower, ROLL, 1), 0.5 * upper))
            folded[pl.ds(pl.multiple_of((v * rows + i) * HALF, HALF), HALF), :] = both
            rest = jnp.sum(jnp.where(f == e + HALF, 0.5 * lower, 0.0), axis=0, keepdims=True)
            corner[pl.ds(v * rows + i, 1), :] = rest

    def first_rows(n, carry):
        for k in range(TOGETHER):
            inner = n * TOGETHER + k
            terms(own * s_dev + inner, own_tile[0, inner])
        return carry

    lax.fori_loop(0, s_dev // TOGETHER, first_rows, 0)
    for there in mates:
        tile_copy(there, there).wait_recv()
        slab_copy(there, there).wait_recv()
        expand(there)
    tile_in[own] = tile_out[...]
    tile_move = pltpu.make_async_copy(tile_in, tile_all, in_sem.at[3])
    tile_move.start()
    tile_move.wait()

    def other_rows(n, carry):
        for k in range(TOGETHER):
            at = n * TOGETHER + k
            there = lax.rem(own + lax.div(at, s_dev), n_row)
            inner = lax.rem(at, s_dev)
            terms(there * s_dev + inner, tile_all[there, 0, inner])
        return carry

    lax.fori_loop(s_dev // TOGETHER, rows // TOGETHER, other_rows, 0)

    near = lax.broadcasted_iota(jnp.int32, (LANES, LANES), 1) < TILE
    chunks = rows // LANES

    def lay(n, carry):
        v = lax.div(n, chunks)
        chunk = lax.rem(n, chunks)
        base = (v * rows + chunk * LANES) * HALF
        for j in range(packed_tiles + 1):
            if j < packed_tiles:
                a = folded[pl.ds(base + 2 * j, LANES, stride=HALF), :]
                b = folded[pl.ds(base + 2 * j + 1, LANES, stride=HALF), :]
            else:
                a = b = corner[pl.ds(pl.multiple_of(v * rows + chunk * LANES, LANES), LANES), :]
            u0 = jnp.where(near, a, pltpu.roll(b, TILE, 1))
            u1 = jnp.where(near, pltpu.roll(a, TILE, 1), b)
            parts = split(u0) + split(u1)
            for k, value in enumerate(parts):
                at = pl.multiple_of(k * rows + chunk * LANES, LANES)
                left[v, pl.ds(at, LANES), j * LANES:(j + 1) * LANES] = value
        return carry

    lax.fori_loop(0, pairs * chunks, lay, 0)

    column = lax.broadcasted_iota(jnp.int32, (LANES, across), 0)
    for r in range(n_row):
        for v in range(pairs):

            def mark(n, carry):
                start = pl.multiple_of(n * LANES, LANES)
                value = jnp.where(column + n * LANES == perm_ref[r, v], 1.0, 0.0)
                hot[r, v, pl.ds(start, LANES), :] = value.astype(jnp.bfloat16)
                return carry

            lax.fori_loop(0, columns // LANES, mark, 0)

    even = lax.rem(lax.broadcasted_iota(jnp.int32, (rows, across), 1), GROUP) < GROUP // 2

    def place(v, r, fresh):
        high, low = split(theirs[v, r])
        value = jnp.concatenate([high, low], axis=0)
        value = lax.dot_general(value, hot[r, v], NT, preferred_element_type=jnp.float32)
        value = value[:s_dev] + value[s_dev:]
        total[...] = value if fresh else total[...] + value

    def place_mates(v):
        for there in mates:
            y_copy(v, there, there).wait_recv()
            place(v, there, False)

    for v in range(pairs):

        def landed(n, carry):
            there = target(n)
            c_copy(v, there, there).wait_recv()
            return carry

        lax.fori_loop(0, n_col - 1, landed, 0)
        both = lax.dot_general(left[v], recv[v], NT, preferred_element_type=jnp.float32)
        u0 = both[:rows] + both[rows:2 * rows]
        u1 = both[2 * rows:3 * rows] + both[3 * rows:]
        value = jnp.where(even, u0, u1)
        for block in range(rows // RB):
            q, r = divmod(block, n_row)
            mine[v, r, q * RB:(q + 1) * RB, :] = value[block * RB:(block + 1) * RB]
        for there in mates:
            y_copy(v, there, own).start()
        theirs[v, own] = mine[v, own]
        place(v, own, v == 0)
        if v > 0:
            place_mates(v - 1)
    place_mates(pairs - 1)

    out_cols = columns // n_col
    for c in range(n_col):
        placed[c] = total[:, c * out_cols:(c + 1) * out_cols]

    def give(n, carry):
        p_copy(target(n), me).start()
        return carry

    lax.fori_loop(0, n_col - 1, give, 0)
    summed = placed[me]
    for k in range(1, n_col):
        there = lax.rem(me + k, n_col)
        p_copy(there, there).wait_recv()
        summed = summed + arrived[there]
    out_ref[...] = summed

    def done(n, carry):
        there = target(n)
        for v in range(pairs):
            c_copy(v, there, me).wait_send()
        p_copy(there, me).wait_send()
        return carry

    lax.fori_loop(0, n_col - 1, done, 0)
    for there in mates:
        tile_copy(there, own).wait_send()
        slab_copy(there, own).wait_send()
        for v in range(pairs):
            y_copy(v, there, own).wait_send()


def body(n_row, n_col, primal, dual_inv, col_values, col_perm, slab_values, slab_tile):
    tile_count = col_values.shape[1]
    order = primal.shape[1]
    columns = col_perm.shape[1]
    s_dev = slab_values.shape[1]
    rows = n_row * s_dev
    keep = col_values.shape[2]
    block = lax.axis_index("col")
    part = tile_count // n_row
    width = part * TILE
    pairs = part // 2
    perm = lax.dynamic_index_in_dim(col_perm, block, 0, keepdims=False)
    perm = perm.reshape(n_row, pairs, 2, n_col, keep)
    perm = jnp.transpose(perm, (0, 1, 3, 2, 4)).reshape(n_row, pairs, 1, n_col * 2 * keep)
    col = col_values.reshape(n_col, tile_count // 2, GROUP, TILE * TILE)

    packed = TILE * TILE // 2 + LANES
    out_cols = columns // n_col
    across = n_col * GROUP
    vmem = pl.BlockSpec(memory_space=pltpu.VMEM)
    whole = pl.BlockSpec(memory_space=pl.ANY)
    dma = pltpu.SemaphoreType.DMA
    f32, bf16, i32 = jnp.float32, jnp.bfloat16, jnp.int32
    return pl.pallas_call(
        functools.partial(kernel, n_row, n_col),
        out_shape=jax.ShapeDtypeStruct((s_dev, out_cols), f32),
        in_specs=[pl.BlockSpec(memory_space=pltpu.SMEM), vmem, vmem, whole, whole, whole, whole],
        out_specs=vmem,
        scratch_shapes=[
            pltpu.VMEM((width, order), f32),
            pltpu.VMEM((order, width), f32),
            pltpu.VMEM((order // TILE, width, 2 * LANES), bf16),
            pltpu.VMEM((order // TILE, 2 * TILE, width), bf16),
            pltpu.VMEM((8, LANES), i32),
            pltpu.VMEM((n_row, 8, LANES), i32),
            pltpu.SMEM((n_row, 8, LANES), i32),
            pltpu.VMEM((n_row, s_dev, TILE * TILE), bf16),
            pltpu.VMEM((rows * TILE, LANES), f32),
            pltpu.VMEM((2, GROUP, TILE * TILE), bf16),
            pltpu.VMEM((n_col, pairs, GROUP, packed), bf16),
            pltpu.VMEM((pairs, across, packed), bf16),
            pltpu.VMEM((pairs * rows * HALF, LANES), f32),
            pltpu.VMEM((pairs * rows, LANES), f32),
            pltpu.VMEM((pairs, 4 * rows, packed), bf16),
            pltpu.VMEM((pairs, n_row, s_dev, across), f32),
            pltpu.VMEM((pairs, n_row, s_dev, across), f32),
            pltpu.VMEM((n_row, pairs, columns, across), bf16),
            pltpu.VMEM((s_dev, columns), f32),
            pltpu.VMEM((n_col, s_dev, out_cols), f32),
            pltpu.VMEM((n_col, s_dev, out_cols), f32),
            dma((2,)), dma((4,)), dma((pairs, n_col)), dma((pairs, n_col)),
            dma((n_row,)), dma((n_row,)), dma((n_row,)), dma((n_row,)),
            dma((pairs, n_row)), dma((pairs, n_row)), dma((n_col,)), dma((n_col,)),
        ],
        compiler_params=pltpu.CompilerParams(
            collective_id=0, has_side_effects=True, vmem_limit_bytes=60 * 1024 * 1024
        ),
    )(slab_tile, slab_tile, perm, primal, dual_inv, slab_values, col)


def solution(mesh):
    def run(*args):
        return body(mesh.shape["row"], mesh.shape["col"], *args)

    return jax.shard_map(
        run,
        mesh=mesh,
        in_specs=(
            P("col", None, None),
            P("col", None, None),
            P(None, None, "col", None),
            P(),
            P("col", "row", None),
            P("col", "row"),
        ),
        out_specs=P("row", "col"),
        check_vma=False,
    )
```

time: 159 us -> 128 us (0.81)
  other arithmetic: 11.1 us -> 0 us
  local copies, waits for them, and re-layouts: 13.5 us -> 3.28 us
  blocking collectives: 5.75 us -> 0 us
  Pallas kernels: 128 us -> 124 us
    concatenate x3 -> x0, other arithmetic: 7.45 us -> none  [the longest x1 4.39 us: body(): x = jnp.concatenate([high, high, low, low], axis=2)]
    all_gather x1 -> x0, blocking collectives: 5.75 us -> none  [body(): tiles = lax.all_gather(slab_tile[0], 'row', axis=0, tiled=True)]
    pallas_call x1, Pallas kernels: 128 us -> 124 us  [body(): pl.pallas_call(functools.partial(kernel, n_row, n_col), out_shape=jax.Sha...]
    convert_element_type x2 -> x0, other arithmetic: 3.68 us -> none  [halves(): return (high.astype(jnp.bfloat16), low.astype(jnp.bfloat16))]
    dynamic_slice x2 -> x0, local copies, waits for them, and re-layouts: 3.36 us -> none  [the longest x1 3.19 us: body(): x = lax.dynamic_slice_in_dim(primal[0], own * width, width, axis=0)]
    unnamed x11 -> x3, local copies, waits for them, and re-layouts: 5.34 us -> 2.28 us
    reshape x3 -> x2, local copies, waits for them, and re-layouts: 3.6 us -> 0.91 us  [the longest x1 0.81 us: body(): jnp.transpose(perm, (0, 1, 3, 2, 4))]
where the time goes in v3:
time: 128 us; the launch traced here: 127 us
  Pallas kernels  124 us (97%)
  local copies, waits for them, and re-layouts  3.28 us (3%)
    pallas_call x1, Pallas kernels, body(): pl.pallas_call(functools.partial(kernel, n_row, n_col), out_shape=jax.Sha...  124 us

profile of v3, /device:TPU:0, one launch (start us, length us, event | category | flops | bytes accessed | tf_op | source)
XLA Modules:
  0.0 127.0 jit_solution(5232296790434624654)
XLA Ops:
  0.0 0.0 copy-start
  0.0 0.9 copy-done
  0.9 0.1 reshape.10
  1.0 0.1 copy.7
  1.1 0.8 reshape.13.perm_ref
  1.9 123.6 %shard_map.64 = f32[64,128]{1,0:T(8,128)} custom-call(s32[1,64]{1,0:T(1,128)} %tile_ref.1, s32[1,64]{1,0:T(1,128)} %tile_ref.1, s32[2,4,1,256]{3,2,1,0:T(1,128)} %reshape.13.perm_ref, f32[1,1024,1024]{2,1,0:T(8,128)} %x_hbm.1, f32[1,1024,1024]{2,1,0:T(8,128)} %z_hbm.1, bf16[1,64,4096]{2,1,0:T(8,128)(2,1)} %s_hbm.1, bf16[16,8,16,4096]{3,2,1,0:T(8,128)(2,1)} %bitcast.2), custom_call_target="tpu_custom_call" | custom-call | tf_op jit(solution)/shard_map/pallas_call | solution.py:362
  125.6 1.4 %copy.10 = f32[64,128]{1,0:T(8,128)} copy(f32[64,128]{1,0:T(8,128)} %shard_map.64) | data formatting | bytes 65536
  (1 shorter events, 0.0 us)
Async XLA Ops:
  0.0 0.9 copy-start

commit v4 on v3

--- a/solution.py
+++ b/solution.py
@@ -14,6 +14,7 @@
 GROUP = 16
 ROLL = LANES - HALF
 TOGETHER = 4
+AHEAD = 16
 MESH = pl.DeviceIdType.MESH
 NT = (((1,), (1,)), ((), ()))
 
@@ -56,13 +57,15 @@
         return lax.rem(me + offset(n), n_col)
 
     def load(n):
-        slot = lax.rem(n, 2)
+        slot = lax.rem(n, AHEAD)
         return pltpu.make_async_copy(
             col_ref.at[target(lax.rem(n, n_col)), own * pairs + lax.div(n, n_col)],
             raw.at[slot], load_sem.at[slot],
         )
 
-    load(0).start()
+    steps = pairs * n_col
+    for n in range(min(AHEAD - 1, steps)):
+        load(n).start()
 
     barrier = pltpu.get_barrier_semaphore()
     for k in range(1, n_col):
@@ -126,12 +129,10 @@
             rest = jnp.where(entry == row + HALF, lower, rest)
         store(packed_tiles, rest.astype(jnp.bfloat16))
 
-    steps = pairs * n_col
-
     def outgoing(n, carry):
-        @pl.when(n + 1 < steps)
+        @pl.when(n + AHEAD - 1 < steps)
         def _():
-            load(n + 1).start()
+            load(n + AHEAD - 1).start()
 
         load(n).wait()
         v = lax.div(n, n_col)
@@ -141,7 +142,7 @@
         def store(j, value):
             send[there, v, :, j * LANES:(j + 1) * LANES] = value
 
-        pack(lax.rem(n, 2), store)
+        pack(lax.rem(n, AHEAD), store)
 
         @pl.when(step < n_col - 1)
         def _():
@@ -195,13 +196,21 @@
         panel = jnp.dot(square, z_ref[t], preferred_element_type=jnp.float32)
         high, low = split(panel)
         right = jnp.concatenate([high, low, high, low], axis=0)
+        done = []
         for v in range(pairs):
             cut = slice(v * LANES, (v + 1) * LANES)
             term = jnp.dot(x_ref[t, cut], right[:, cut], preferred_element_type=jnp.float32)
-            term = term.astype(jnp.bfloat16).astype(jnp.float32)
-            term = term + term.T
             term = jnp.where(first, term[:TILE], term[TILE:])
-            upper, lower = term[:HALF], term[HALF:]
+            done.append(term.astype(jnp.bfloat16).astype(jnp.float32))
+        if pairs % 2:
+            done.append(done[-1])
+        for v in range(0, len(done), 2):
+            turned = jnp.concatenate(done[v:v + 2], axis=0).T
+            crossed = pltpu.roll(turned, TILE, 1)
+            done[v] += jnp.where(first, turned[:TILE], crossed[TILE:])
+            done[v + 1] += jnp.where(first, crossed[:TILE], turned[TILE:])
+        for v in range(pairs):
+            upper, lower = done[v][:HALF], done[v][HALF:]
             both = jnp.where(f > e, upper, jnp.where(f < e, pltpu.roll(lower, ROLL, 1), 0.5 * upper))
             folded[pl.ds(pl.multiple_of((v * rows + i) * HALF, HALF), HALF), :] = both
             rest = jnp.sum(jnp.where(f == e + HALF, 0.5 * lower, 0.0), axis=0, keepdims=True)
@@ -374,7 +383,7 @@
             pltpu.SMEM((n_row, 8, LANES), i32),
             pltpu.VMEM((n_row, s_dev, TILE * TILE), bf16),
             pltpu.VMEM((rows * TILE, LANES), f32),
-            pltpu.VMEM((2, GROUP, TILE * TILE), bf16),
+            pltpu.VMEM((AHEAD, GROUP, TILE * TILE), bf16),
             pltpu.VMEM((n_col, pairs, GROUP, packed), bf16),
             pltpu.VMEM((pairs, across, packed), bf16),
             pltpu.VMEM((pairs * rows * HALF, LANES), f32),
@@ -386,7 +395,7 @@
             pltpu.VMEM((s_dev, columns), f32),
             pltpu.VMEM((n_col, s_dev, out_cols), f32),
             pltpu.VMEM((n_col, s_dev, out_cols), f32),
-            dma((2,)), dma((4,)), dma((pairs, n_col)), dma((pairs, n_col)),
+            dma((AHEAD,)), dma((4,)), dma((pairs, n_col)), dma((pairs, n_col)),
             dma((n_row,)), dma((n_row,)), dma((n_row,)), dma((n_row,)),
             dma((pairs, n_row)), dma((pairs, n_row)), dma((n_col,)), dma((n_col,)),
         ],

time: 128 us -> 125 us (0.977)
  Pallas kernels: 124 us -> 122 us
    pallas_call x1, Pallas kernels: 124 us -> 122 us  [body(): pl.pallas_call(functools.partial(kernel, n_row, n_col), out_shape=jax.Sha...]
where the time goes in v4:
time: 125 us
  Pallas kernels  122 us (98%)
  local copies, waits for them, and re-layouts  3.28 us (3%)
    pallas_call x1, Pallas kernels, body(): pl.pallas_call(functools.partial(kernel, n_row, n_col), out_shape=jax.Sha...  122 us

profile of v4, /device:TPU:0, one launch (start us, length us, event | category | flops | bytes accessed | tf_op | source)
XLA Modules:
  0.0 125.1 jit_solution(17684616507369594046)
XLA Ops:
  0.0 0.0 copy-start
  0.0 0.9 copy-done
  0.9 0.1 reshape.10
  1.0 0.1 copy.7
  1.1 0.8 reshape.13.perm_ref
  1.9 121.8 %shard_map.64 = f32[64,128]{1,0:T(8,128)} custom-call(s32[1,64]{1,0:T(1,128)} %tile_ref.1, s32[1,64]{1,0:T(1,128)} %tile_ref.1, s32[2,4,1,256]{3,2,1,0:T(1,128)} %reshape.13.perm_ref, f32[1,1024,1024]{2,1,0:T(8,128)} %x_hbm.1, f32[1,1024,1024]{2,1,0:T(8,128)} %z_hbm.1, bf16[1,64,4096]{2,1,0:T(8,128)(2,1)} %s_hbm.1, bf16[16,8,16,4096]{3,2,1,0:T(8,128)(2,1)} %bitcast.2), custom_call_target="tpu_custom_call" | custom-call | tf_op jit(solution)/shard_map/pallas_call | solution.py:371
  123.8 1.4 %copy.10 = f32[64,128]{1,0:T(8,128)} copy(f32[64,128]{1,0:T(8,128)} %shard_map.64) | data formatting | bytes 65536
  (1 shorter events, 0.0 us)
Async XLA Ops:
  0.0 0.9 copy-start

commit v5 on v4

--- a/solution.py
+++ b/solution.py
@@ -50,11 +50,14 @@
     z_copy.start()
     s_copy.start()
 
-    def offset(n):
-        return n_col // 2 + lax.div(n + 1, 2) * (1 - 2 * lax.rem(n, 2))
+    half_col = n_col // 2
+    my_half = lax.div(me, half_col)
+    my_place = lax.rem(me, half_col)
 
     def target(n):
-        return lax.rem(me + offset(n), n_col)
+        near = lax.rem(n, 2)
+        side = near * my_half + (1 - near) * (1 - my_half)
+        return side * half_col + lax.rem(my_place + lax.div(n + 1, 2), half_col)
 
     def load(n):
         slot = lax.rem(n, AHEAD)

time: 125 us -> 127 us (1.016)
  Pallas kernels: 122 us -> 124 us
    pallas_call x1, Pallas kernels: 122 us -> 124 us  [body(): pl.pallas_call(functools.partial(kernel, n_row, n_col), out_shape=jax.Sha...]
where the time goes in v5:
time: 127 us
  Pallas kernels  124 us (98%)
  local copies, waits for them, and re-layouts  3.28 us (3%)
    pallas_call x1, Pallas kernels, body(): pl.pallas_call(functools.partial(kernel, n_row, n_col), out_shape=jax.Sha...  124 us

profile of v5, /device:TPU:0, one launch (start us, length us, event | category | flops | bytes accessed | tf_op | source)
XLA Modules:
  0.0 127.0 jit_solution(85278563990978510)
XLA Ops:
  0.0 0.0 copy-start
  0.0 0.9 copy-done
  0.9 0.1 reshape.10
  1.0 0.1 copy.7
  1.1 0.8 reshape.13.perm_ref
  1.9 123.7 %shard_map.64 = f32[64,128]{1,0:T(8,128)} custom-call(s32[1,64]{1,0:T(1,128)} %tile_ref.1, s32[1,64]{1,0:T(1,128)} %tile_ref.1, s32[2,4,1,256]{3,2,1,0:T(1,128)} %reshape.13.perm_ref, f32[1,1024,1024]{2,1,0:T(8,128)} %x_hbm.1, f32[1,1024,1024]{2,1,0:T(8,128)} %z_hbm.1, bf16[1,64,4096]{2,1,0:T(8,128)(2,1)} %s_hbm.1, bf16[16,8,16,4096]{3,2,1,0:T(8,128)(2,1)} %bitcast.2), custom_call_target="tpu_custom_call" | custom-call | tf_op jit(solution)/shard_map/pallas_call | solution.py:374
  125.6 1.4 %copy.10 = f32[64,128]{1,0:T(8,128)} copy(f32[64,128]{1,0:T(8,128)} %shard_map.64) | data formatting | bytes 65536
  (1 shorter events, 0.0 us)
Async XLA Ops:
  0.0 0.9 copy-start

commit v6 on v4

--- a/solution.py
+++ b/solution.py
@@ -28,8 +28,8 @@
 def kernel(
     n_row, n_col, own_tile, tile_ref, perm_ref, x_hbm, z_hbm, s_hbm, col_ref, out_ref,
     x_raw, z_raw, x_ref, z_ref, tile_out, tile_in, tile_all, s_raw, slab,
-    raw, send, recv, folded, corner, left, mine, theirs, hot, total, placed, arrived,
-    load_sem, in_sem, c_send, c_recv, s_send, s_recv, t_send, t_recv, y_send, y_recv, p_send, p_recv,
+    raw, send, recv, folded, corner, left, mine, theirs, hot, total, placed, arrived, over_out, over_in,
+    load_sem, in_sem, c_send, c_recv, s_send, s_recv, t_send, t_recv, y_send, y_recv, p_send, p_recv, o_send, o_recv,
 ):
     me = lax.axis_index("col")
     own = lax.axis_index("row")
@@ -101,12 +101,23 @@
             device_id={"col": there}, device_id_type=MESH,
         )
 
-    def p_copy(there, here):
+    half_col = n_col // 2
+    my_side = lax.div(me, half_col)
+    my_place = lax.rem(me, half_col)
+    far_side = 1 - my_side
+    sides = (far_side, my_side)
+
+    def p_copy(which, there, here):
         return pltpu.make_async_remote_copy(
-            src_ref=placed.at[there], dst_ref=arrived.at[here],
-            send_sem=p_send.at[there], recv_sem=p_recv.at[here],
-            device_id={"col": there}, device_id_type=MESH,
+            src_ref=placed.at[sides[which] * half_col + there], dst_ref=arrived.at[which, here],
+            send_sem=p_send.at[which, there], recv_sem=p_recv.at[which, here],
+            device_id={"col": my_side * half_col + there}, device_id_type=MESH,
         )
+
+    over_copy = pltpu.make_async_remote_copy(
+        src_ref=over_out, dst_ref=over_in, send_sem=o_send.at[0], recv_sem=o_recv.at[0],
+        device_id={"col": far_side * half_col + my_place}, device_id_type=MESH,
+    )
 
     mates = [lax.rem(own + k, n_row) for k in range(1, n_row)]
     for there in mates:
@@ -318,23 +329,31 @@
     for c in range(n_col):
         placed[c] = total[:, c * out_cols:(c + 1) * out_cols]
 
-    def give(n, carry):
-        p_copy(target(n), me).start()
-        return carry
-
-    lax.fori_loop(0, n_col - 1, give, 0)
+    near_ones = [lax.rem(my_place + k, half_col) for k in range(1, half_col)]
+    for which in range(2):
+        for there in near_ones:
+            p_copy(which, there, my_place).start()
+    summed = placed[far_side * half_col + my_place]
+    for there in near_ones:
+        p_copy(0, there, there).wait_recv()
+        summed = summed + arrived[0, there]
+    over_out[...] = summed
+    over_copy.start()
     summed = placed[me]
-    for k in range(1, n_col):
-        there = lax.rem(me + k, n_col)
-        p_copy(there, there).wait_recv()
-        summed = summed + arrived[there]
-    out_ref[...] = summed
+    for there in near_ones:
+        p_copy(1, there, there).wait_recv()
+        summed = summed + arrived[1, there]
+    over_copy.wait_recv()
+    out_ref[...] = summed + over_in[...]
+    over_copy.wait_send()
+    for which in range(2):
+        for there in near_ones:
+            p_copy(which, there, my_place).wait_send()
 
     def done(n, carry):
         there = target(n)
         for v in range(pairs):
             c_copy(v, there, me).wait_send()
-        p_copy(there, me).wait_send()
         return carry
 
     lax.fori_loop(0, n_col - 1, done, 0)
@@ -394,10 +413,13 @@
             pltpu.VMEM((n_row, pairs, columns, across), bf16),
             pltpu.VMEM((s_dev, columns), f32),
             pltpu.VMEM((n_col, s_dev, out_cols), f32),
-            pltpu.VMEM((n_col, s_dev, out_cols), f32),
+            pltpu.VMEM((2, n_col // 2, s_dev, out_cols), f32),
+            pltpu.VMEM((s_dev, out_cols), f32),
+            pltpu.VMEM((s_dev, out_cols), f32),
             dma((AHEAD,)), dma((4,)), dma((pairs, n_col)), dma((pairs, n_col)),
             dma((n_row,)), dma((n_row,)), dma((n_row,)), dma((n_row,)),
-            dma((pairs, n_row)), dma((pairs, n_row)), dma((n_col,)), dma((n_col,)),
+            dma((pairs, n_row)), dma((pairs, n_row)), dma((2, n_col // 2)), dma((2, n_col // 2)),
+            dma((1,)), dma((1,)),
         ],
         compiler_params=pltpu.CompilerParams(
             collective_id=0, has_side_effects=True, vmem_limit_bytes=60 * 1024 * 1024

time: 125 us -> 122 us (0.976)
  Pallas kernels: 122 us -> 118 us
    pallas_call x1, Pallas kernels: 122 us -> 118 us  [body(): pl.pallas_call(functools.partial(kernel, n_row, n_col), out_shape=jax.Sha...]
where the time goes in v6:
time: 122 us
  Pallas kernels  118 us (97%)
  local copies, waits for them, and re-layouts  3.28 us (3%)
    pallas_call x1, Pallas kernels, body(): pl.pallas_call(functools.partial(kernel, n_row, n_col), out_shape=jax.Sha...  118 us

profile of v6, /device:TPU:0, one launch (start us, length us, event | category | flops | bytes accessed | tf_op | source)
XLA Modules:
  0.0 121.7 jit_solution(15984711266672131828)
XLA Ops:
  0.0 0.0 copy-start
  0.0 0.9 copy-done
  0.9 0.1 reshape.10
  1.0 0.1 copy.7
  1.1 0.8 reshape.13.perm_ref
  1.9 118.4 %shard_map.64 = f32[64,128]{1,0:T(8,128)} custom-call(s32[1,64]{1,0:T(1,128)} %tile_ref.1, s32[1,64]{1,0:T(1,128)} %tile_ref.1, s32[2,4,1,256]{3,2,1,0:T(1,128)} %reshape.13.perm_ref, f32[1,1024,1024]{2,1,0:T(8,128)} %x_hbm.1, f32[1,1024,1024]{2,1,0:T(8,128)} %z_hbm.1, bf16[1,64,4096]{2,1,0:T(8,128)(2,1)} %s_hbm.1, bf16[16,8,16,4096]{3,2,1,0:T(8,128)(2,1)} %bitcast.2), custom_call_target="tpu_custom_call" | custom-call | tf_op jit(solution)/shard_map/pallas_call | solution.py:390
  120.3 1.4 %copy.10 = f32[64,128]{1,0:T(8,128)} copy(f32[64,128]{1,0:T(8,128)} %shard_map.64) | data formatting | bytes 65536
  (1 shorter events, 0.0 us)
Async XLA Ops:
  0.0 0.9 copy-start

commit v7 on v6

--- a/solution.py
+++ b/solution.py
@@ -29,7 +29,8 @@
     n_row, n_col, own_tile, tile_ref, perm_ref, x_hbm, z_hbm, s_hbm, col_ref, out_ref,
     x_raw, z_raw, x_ref, z_ref, tile_out, tile_in, tile_all, s_raw, slab,
     raw, send, recv, folded, corner, left, mine, theirs, hot, total, placed, arrived, over_out, over_in,
-    load_sem, in_sem, c_send, c_recv, s_send, s_recv, t_send, t_recv, y_send, y_recv, p_send, p_recv, o_send, o_recv,
+    rest_sum, rest_out, rest_in,
+    load_sem, in_sem, c_send, c_recv, s_send, s_recv, t_send, t_recv, y_send, y_recv, p_send, p_recv, o_send, o_recv, r_send, r_recv,
 ):
     me = lax.axis_index("col")
     own = lax.axis_index("row")
@@ -138,32 +139,61 @@
             both = jnp.where(entry >= row, upper, pltpu.roll(lower, ROLL, 1))
             store(j, both.astype(jnp.bfloat16))
             rest = jnp.where(entry == row + HALF, lower, rest)
-        store(packed_tiles, rest.astype(jnp.bfloat16))
-
-    def outgoing(n, carry):
-        @pl.when(n + AHEAD - 1 < steps)
-        def _():
-            load(n + AHEAD - 1).start()
-
-        load(n).wait()
-        v = lax.div(n, n_col)
-        step = lax.rem(n, n_col)
-        there = target(step)
-
-        def store(j, value):
-            send[there, v, :, j * LANES:(j + 1) * LANES] = value
-
-        pack(lax.rem(n, AHEAD), store)
-
-        @pl.when(step < n_col - 1)
-        def _():
-            c_copy(v, there, me).start()
-
+        return rest
+
+    def r_copy(there, here):
+        return pltpu.make_async_remote_copy(
+            src_ref=rest_out.at[there], dst_ref=rest_in.at[pl.ds(here * GROUP, GROUP)],
+            send_sem=r_send.at[there], recv_sem=r_recv.at[here],
+            device_id={"col": there}, device_id_type=MESH,
+        )
+
+    for v in range(pairs):
+
+        def outgoing(step, carry):
+            n = v * n_col + step
+
+            @pl.when(n + AHEAD - 1 < steps)
+            def _():
+                load(n + AHEAD - 1).start()
+
+            load(n).wait()
+            there = target(step)
+
+            def store(j, value):
+                send[there, v, :, j * LANES:(j + 1) * LANES] = value
+
+            rest = pack(lax.rem(n, AHEAD), store)
+            if v == 0:
+                rest_sum[there] = rest
+
+                @pl.when(step < n_col - 1)
+                def _():
+                    c_copy(v, there, me).start()
+            else:
+                rest_sum[there] += pltpu.roll(rest, v * HALF, 1)
+            return carry
+
+        lax.fori_loop(0, n_col, outgoing, 0)
+
+    rest_out[...] = rest_sum[...].astype(jnp.bfloat16)
+
+    def rests(step, carry):
+        r_copy(target(step), me).start()
         return carry
 
-    lax.fori_loop(0, steps, outgoing, 0)
+    lax.fori_loop(0, n_col - 1, rests, 0)
+    for v in range(1, pairs):
+
+        def later(step, carry):
+            c_copy(v, target(step), me).start()
+            return carry
+
+        lax.fori_loop(0, n_col - 1, later, 0)
+    my_rows = pl.ds(pl.multiple_of(me * GROUP, GROUP), GROUP)
     for v in range(pairs):
-        recv[v, pl.ds(pl.multiple_of(me * GROUP, GROUP), GROUP), :] = send[me, v]
+        recv[v, my_rows, :] = send[me, v]
+    rest_in[my_rows, :] = rest_out[me]
 
     half = lax.broadcasted_iota(jnp.int32, (width, LANES), 1) < TILE
     x_copy.wait()
@@ -253,28 +283,34 @@
 
     lax.fori_loop(s_dev // TOGETHER, rows // TOGETHER, other_rows, 0)
 
-    near = lax.broadcasted_iota(jnp.int32, (LANES, LANES), 1) < TILE
-    chunks = rows // LANES
-
-    def lay(n, carry):
-        v = lax.div(n, chunks)
-        chunk = lax.rem(n, chunks)
-        base = (v * rows + chunk * LANES) * HALF
-        for j in range(packed_tiles + 1):
-            if j < packed_tiles:
-                a = folded[pl.ds(base + 2 * j, LANES, stride=HALF), :]
-                b = folded[pl.ds(base + 2 * j + 1, LANES, stride=HALF), :]
-            else:
-                a = b = corner[pl.ds(pl.multiple_of(v * rows + chunk * LANES, LANES), LANES), :]
-            u0 = jnp.where(near, a, pltpu.roll(b, TILE, 1))
-            u1 = jnp.where(near, pltpu.roll(a, TILE, 1), b)
-            parts = split(u0) + split(u1)
-            for k, value in enumerate(parts):
-                at = pl.multiple_of(k * rows + chunk * LANES, LANES)
-                left[v, pl.ds(at, LANES), j * LANES:(j + 1) * LANES] = value
-        return carry
-
-    lax.fori_loop(0, pairs * chunks, lay, 0)
+    spot = lax.broadcasted_iota(jnp.int32, (LANES, LANES), 1)
+    near = spot < TILE
+    parity = jnp.where(near, 0, 1) == lax.rem(spot, 2)
+    for v in range(pairs):
+
+        def lay(chunk, carry):
+            base = (v * rows + chunk * LANES) * HALF
+            for j in range(packed_tiles + 1):
+                if j < packed_tiles:
+                    a = folded[pl.ds(base + 2 * j, LANES, stride=HALF), :]
+                    b = folded[pl.ds(base + 2 * j + 1, LANES, stride=HALF), :]
+                else:
+                    a = b = corner[pl.ds(pl.multiple_of(v * rows + chunk * LANES, LANES), LANES), :]
+                u0 = jnp.where(near, a, pltpu.roll(b, TILE, 1))
+                u1 = jnp.where(near, pltpu.roll(a, TILE, 1), b)
+                if j == packed_tiles:
+                    u0 = jnp.where(parity, u0, 0.0)
+                    u1 = jnp.where(parity, u1, 0.0)
+                    if v:
+                        u0 = pltpu.roll(u0, v * HALF, 1)
+                        u1 = pltpu.roll(u1, v * HALF, 1)
+                parts = split(u0) + split(u1)
+                for k, value in enumerate(parts):
+                    at = pl.multiple_of(k * rows + chunk * LANES, LANES)
+                    left[v, pl.ds(at, LANES), j * LANES:(j + 1) * LANES] = value
+            return carry
+
+        lax.fori_loop(0, rows // LANES, lay, 0)
 
     column = lax.broadcasted_iota(jnp.int32, (LANES, across), 0)
     for r in range(n_row):
@@ -307,10 +343,14 @@
         def landed(n, carry):
             there = target(n)
             c_copy(v, there, there).wait_recv()
+            if v == 0:
+                r_copy(there, there).wait_recv()
             return carry
 
         lax.fori_loop(0, n_col - 1, landed, 0)
-        both = lax.dot_general(left[v], recv[v], NT, preferred_element_type=jnp.float32)
+        most = packed_tiles * LANES
+        both = lax.dot_general(left[v, :, :most], recv[v], NT, preferred_element_type=jnp.float32)
+        both += lax.dot_general(left[v, :, most:], rest_in[...], NT, preferred_element_type=jnp.float32)
         u0 = both[:rows] + both[rows:2 * rows]
         u1 = both[2 * rows:3 * rows] + both[3 * rows:]
         value = jnp.where(even, u0, u1)
@@ -354,6 +394,7 @@
         there = target(n)
         for v in range(pairs):
             c_copy(v, there, me).wait_send()
+        r_copy(there, me).wait_send()
         return carry
 
     lax.fori_loop(0, n_col - 1, done, 0)
@@ -403,8 +444,8 @@
             pltpu.VMEM((n_row, s_dev, TILE * TILE), bf16),
             pltpu.VMEM((rows * TILE, LANES), f32),
             pltpu.VMEM((AHEAD, GROUP, TILE * TILE), bf16),
-            pltpu.VMEM((n_col, pairs, GROUP, packed), bf16),
-            pltpu.VMEM((pairs, across, packed), bf16),
+            pltpu.VMEM((n_col, pairs, GROUP, packed - LANES), bf16),
+            pltpu.VMEM((pairs, across, packed - LANES), bf16),
             pltpu.VMEM((pairs * rows * HALF, LANES), f32),
             pltpu.VMEM((pairs * rows, LANES), f32),
             pltpu.VMEM((pairs, 4 * rows, packed), bf16),
@@ -416,10 +457,13 @@
             pltpu.VMEM((2, n_col // 2, s_dev, out_cols), f32),
             pltpu.VMEM((s_dev, out_cols), f32),
             pltpu.VMEM((s_dev, out_cols), f32),
+            pltpu.VMEM((n_col, GROUP, LANES), f32),
+            pltpu.VMEM((n_col, GROUP, LANES), bf16),
+            pltpu.VMEM((across, LANES), bf16),
             dma((AHEAD,)), dma((4,)), dma((pairs, n_col)), dma((pairs, n_col)),
             dma((n_row,)), dma((n_row,)), dma((n_row,)), dma((n_row,)),
             dma((pairs, n_row)), dma((pairs, n_row)), dma((2, n_col // 2)), dma((2, n_col // 2)),
-            dma((1,)), dma((1,)),
+            dma((1,)), dma((1,)), dma((n_col,)), dma((n_col,)),
         ],
         compiler_params=pltpu.CompilerParams(
             collective_id=0, has_side_effects=True, vmem_limit_bytes=60 * 1024 * 1024

time: 122 us -> 118 us (0.967)
  Pallas kernels: 118 us -> 114 us
    pallas_call x1, Pallas kernels: 118 us -> 114 us  [body(): pl.pallas_call(functools.partial(kernel, n_row, n_col), out_shape=jax.Sha...]
where the time goes in v7:
time: 118 us
  Pallas kernels  114 us (97%)
  local copies, waits for them, and re-layouts  3.28 us (3%)
    pallas_call x1, Pallas kernels, body(): pl.pallas_call(functools.partial(kernel, n_row, n_col), out_shape=jax.Sha...  114 us

profile of v7, /device:TPU:0, one launch (start us, length us, event | category | flops | bytes accessed | tf_op | source)
XLA Modules:
  0.0 117.7 jit_solution(10677303720098852472)
XLA Ops:
  0.0 0.0 copy-start
  0.0 0.9 copy-done
  0.9 0.1 reshape.10
  1.0 0.1 copy.7
  1.1 0.8 reshape.13.perm_ref
  1.9 114.4 %shard_map.64 = f32[64,128]{1,0:T(8,128)} custom-call(s32[1,64]{1,0:T(1,128)} %tile_ref.1, s32[1,64]{1,0:T(1,128)} %tile_ref.1, s32[2,4,1,256]{3,2,1,0:T(1,128)} %reshape.13.perm_ref, f32[1,1024,1024]{2,1,0:T(8,128)} %x_hbm.1, f32[1,1024,1024]{2,1,0:T(8,128)} %z_hbm.1, bf16[1,64,4096]{2,1,0:T(8,128)(2,1)} %s_hbm.1, bf16[16,8,16,4096]{3,2,1,0:T(8,128)(2,1)} %bitcast.2), custom_call_target="tpu_custom_call" | custom-call | tf_op jit(solution)/shard_map/pallas_call | solution.py:431
  116.3 1.4 %copy.10 = f32[64,128]{1,0:T(8,128)} copy(f32[64,128]{1,0:T(8,128)} %shard_map.64) | data formatting | bytes 65536
  (1 shorter events, 0.0 us)
Async XLA Ops:
  0.0 0.9 copy-start

commit v8 on v7

--- a/solution.py
+++ b/solution.py
@@ -26,10 +26,10 @@
 
 
 def kernel(
-    n_row, n_col, own_tile, tile_ref, perm_ref, x_hbm, z_hbm, s_hbm, col_ref, out_ref,
+    n_row, n_col, own_tile, tile_ref, perm_hbm, x_hbm, z_hbm, s_hbm, col_ref, out_ref,
     x_raw, z_raw, x_ref, z_ref, tile_out, tile_in, tile_all, s_raw, slab,
     raw, send, recv, folded, corner, left, mine, theirs, hot, total, placed, arrived, over_out, over_in,
-    rest_sum, rest_out, rest_in,
+    rest_sum, rest_out, rest_in, perm_raw, perm_ref,
     load_sem, in_sem, c_send, c_recv, s_send, s_recv, t_send, t_recv, y_send, y_recv, p_send, p_recv, o_send, o_recv, r_send, r_recv,
 ):
     me = lax.axis_index("col")
@@ -50,6 +50,8 @@
     x_copy.start()
     z_copy.start()
     s_copy.start()
+    perm_copy = pltpu.make_async_copy(perm_hbm.at[pl.ds(me, 1)], perm_raw, in_sem.at[4])
+    perm_copy.start()
 
     def offset(n):
         return n_col // 2 + lax.div(n + 1, 2) * (1 - 2 * lax.rem(n, 2))
@@ -312,6 +314,22 @@
 
         lax.fori_loop(0, rows // LANES, lay, 0)
 
+    perm_copy.wait()
+    keep = GROUP // 2
+    group = lax.div(lax.broadcasted_iota(jnp.int32, (1, LANES), 1), keep)
+    for r in range(n_row):
+        for v in range(pairs):
+            for h in range(across // LANES):
+                value = jnp.zeros((1, LANES), jnp.int32)
+                for g in range(LANES // keep):
+                    start = ((r * pairs + v) * 2 + g % 2) * (across // 2)
+                    old = (h * (LANES // GROUP) + g // 2) * keep
+                    turn = (g * keep - old) % LANES
+                    piece = perm_raw[:, start:start + LANES]
+                    piece = pltpu.roll(piece, turn, 1) if turn else piece
+                    value = jnp.where(group == g, piece, value)
+                perm_ref[r, v, :, h * LANES:(h + 1) * LANES] = value
+
     column = lax.broadcasted_iota(jnp.int32, (LANES, across), 0)
     for r in range(n_row):
         for v in range(pairs):
@@ -339,6 +357,8 @@
             place(v, there, False)
 
     for v in range(pairs):
+        if v > 0:
+            place_mates(v - 1)
 
         def landed(n, carry):
             there = target(n)
@@ -361,9 +381,8 @@
             y_copy(v, there, own).start()
         theirs[v, own] = mine[v, own]
         place(v, own, v == 0)
-        if v > 0:
-            place_mates(v - 1)
-    place_mates(pairs - 1)
+        if v == pairs - 1:
+            place_mates(v)
 
     out_cols = columns // n_col
     for c in range(n_col):
@@ -412,13 +431,9 @@
     s_dev = slab_values.shape[1]
     rows = n_row * s_dev
     keep = col_values.shape[2]
-    block = lax.axis_index("col")
     part = tile_count // n_row
     width = part * TILE
     pairs = part // 2
-    perm = lax.dynamic_index_in_dim(col_perm, block, 0, keepdims=False)
-    perm = perm.reshape(n_row, pairs, 2, n_col, keep)
-    perm = jnp.transpose(perm, (0, 1, 3, 2, 4)).reshape(n_row, pairs, 1, n_col * 2 * keep)
     col = col_values.reshape(n_col, tile_count // 2, GROUP, TILE * TILE)
 
     packed = TILE * TILE // 2 + LANES
@@ -431,7 +446,7 @@
     return pl.pallas_call(
         functools.partial(kernel, n_row, n_col),
         out_shape=jax.ShapeDtypeStruct((s_dev, out_cols), f32),
-        in_specs=[pl.BlockSpec(memory_space=pltpu.SMEM), vmem, vmem, whole, whole, whole, whole],
+        in_specs=[pl.BlockSpec(memory_space=pltpu.SMEM), vmem, whole, whole, whole, whole, whole],
         out_specs=vmem,
         scratch_shapes=[
             pltpu.VMEM((width, order), f32),
@@ -460,7 +475,9 @@
             pltpu.VMEM((n_col, GROUP, LANES), f32),
             pltpu.VMEM((n_col, GROUP, LANES), bf16),
             pltpu.VMEM((across, LANES), bf16),
-            dma((AHEAD,)), dma((4,)), dma((pairs, n_col)), dma((pairs, n_col)),
+            pltpu.VMEM((1, columns), i32),
+            pltpu.VMEM((n_row, pairs, 1, across), i32),
+            dma((AHEAD,)), dma((5,)), dma((pairs, n_col)), dma((pairs, n_col)),
             dma((n_row,)), dma((n_row,)), dma((n_row,)), dma((n_row,)),
             dma((pairs, n_row)), dma((pairs, n_row)), dma((2, n_col // 2)), dma((2, n_col // 2)),
             dma((1,)), dma((1,)), dma((n_col,)), dma((n_col,)),
@@ -468,7 +485,7 @@
         compiler_params=pltpu.CompilerParams(
             collective_id=0, has_side_effects=True, vmem_limit_bytes=60 * 1024 * 1024
         ),
-    )(slab_tile, slab_tile, perm, primal, dual_inv, slab_values, col)
+    )(slab_tile, slab_tile, col_perm, primal, dual_inv, slab_values, col)
 
 
 def solution(mesh):

time: 118 us -> 116 us (0.983)
  local copies, waits for them, and re-layouts: 3.28 us -> 1.38 us
where the time goes in v8:
time: 116 us
  Pallas kernels  114 us (98%)
  local copies, waits for them, and re-layouts  1.38 us (1%)
    pallas_call x1, Pallas kernels, body(): pl.pallas_call(functools.partial(kernel, n_row, n_col), out_shape=jax.Sha...  114 us

profile of v8, /device:TPU:0, one launch (start us, length us, event | category | flops | bytes accessed | tf_op | source)
XLA Modules:
  0.0 115.7 jit_solution(4750987874387242418)
XLA Ops:
  0.0 114.4 %shard_map.64 = f32[64,128]{1,0:T(8,128)} custom-call(s32[1,64]{1,0:T(1,128)} %tile_ref.1, s32[1,64]{1,0:T(1,128)} %tile_ref.1, s32[16,2048]{1,0:T(8,128)} %perm_hbm.1, f32[1,1024,1024]{2,1,0:T(8,128)} %x_hbm.1, f32[1,1024,1024]{2,1,0:T(8,128)} %z_hbm.1, bf16[1,64,4096]{2,1,0:T(8,128)(2,1)} %s_hbm.1, bf16[16,8,16,4096]{3,2,1,0:T(8,128)(2,1)} %bitcast.1), custom_call_target="tpu_custom_call" | custom-call | tf_op jit(solution)/shard_map/pallas_call | solution.py:446
  114.4 1.4 %copy.8 = f32[64,128]{1,0:T(8,128)} copy(f32[64,128]{1,0:T(8,128)} %shard_map.64) | data formatting | bytes 65536

commit v9 on v8

--- a/solution.py
+++ b/solution.py
@@ -47,17 +47,11 @@
         z_hbm.at[0, :, pl.ds(pl.multiple_of(own * width, LANES), width)], z_raw, in_sem.at[1]
     )
     s_copy = pltpu.make_async_copy(s_hbm.at[0], s_raw.at[own], in_sem.at[2])
-    x_copy.start()
-    z_copy.start()
-    s_copy.start()
     perm_copy = pltpu.make_async_copy(perm_hbm.at[pl.ds(me, 1)], perm_raw, in_sem.at[4])
-    perm_copy.start()
-
-    def offset(n):
-        return n_col // 2 + lax.div(n + 1, 2) * (1 - 2 * lax.rem(n, 2))
 
     def target(n):
-        return lax.rem(me + offset(n), n_col)
+        side = lax.rem(lax.div(me, n_col // 2) + 1 + lax.div(n, n_col // 2), 2)
+        return side * (n_col // 2) + lax.rem(me + 1 + n, n_col // 2)
 
     def load(n):
         slot = lax.rem(n, AHEAD)
@@ -69,6 +63,10 @@
     steps = pairs * n_col
     for n in range(min(AHEAD - 1, steps)):
         load(n).start()
+    x_copy.start()
+    z_copy.start()
+    s_copy.start()
+    perm_copy.start()
 
     barrier = pltpu.get_barrier_semaphore()
     for k in range(1, n_col):

time: 116 us -> 118 us (1.017)
  Pallas kernels: 114 us -> 116 us
    pallas_call x1, Pallas kernels: 114 us -> 116 us  [body(): pl.pallas_call(functools.partial(kernel, n_row, n_col), out_shape=jax.Sha...]
where the time goes in v9:
time: 118 us
  Pallas kernels  116 us (98%)
  local copies, waits for them, and re-layouts  1.38 us (1%)
    pallas_call x1, Pallas kernels, body(): pl.pallas_call(functools.partial(kernel, n_row, n_col), out_shape=jax.Sha...  116 us

profile of v9, /device:TPU:0, one launch (start us, length us, event | category | flops | bytes accessed | tf_op | source)
XLA Modules:
  0.0 117.8 jit_solution(13096528090812695153)
XLA Ops:
  0.0 116.4 %shard_map.64 = f32[64,128]{1,0:T(8,128)} custom-call(s32[1,64]{1,0:T(1,128)} %tile_ref.1, s32[1,64]{1,0:T(1,128)} %tile_ref.1, s32[16,2048]{1,0:T(8,128)} %perm_hbm.1, f32[1,1024,1024]{2,1,0:T(8,128)} %x_hbm.1, f32[1,1024,1024]{2,1,0:T(8,128)} %z_hbm.1, bf16[1,64,4096]{2,1,0:T(8,128)(2,1)} %s_hbm.1, bf16[16,8,16,4096]{3,2,1,0:T(8,128)(2,1)} %bitcast.1), custom_call_target="tpu_custom_call" | custom-call | tf_op jit(solution)/shard_map/pallas_call | solution.py:444
  116.4 1.4 %copy.8 = f32[64,128]{1,0:T(8,128)} copy(f32[64,128]{1,0:T(8,128)} %shard_map.64) | data formatting | bytes 65536
